TPU v7x, 32 devices: a whole 2x2x4 slice. The times are simulated.
32 devices in a mesh: dp: 4 (over y, core), mp: 8 (over z, x).
Axes of the slice: x: 2, y: 2, z: 4, core: 2. Of those that a mesh axis runs over, the one named last changes fastest.
Arguments:
- tokens: bfloat16 [512, 8192], P('dp', 'mp'), may hold values from -6 to 6
- cotangent: bfloat16 [512, 28672], P('dp', 'mp'), may hold values from -2 to 2
- tiles: bfloat16 [2, 1344, 128, 128], P(None, 'mp'), may hold values from -0.1875 to 0.1875
- tile_rows: int32 [2, 1344], replicated, may hold values from 0 to 63, as said below
- tile_cols: int32 [2, 1344], replicated, may hold values from 0 to 223, as said below
Outputs:
- hidden: bfloat16 [512, 28672], P('dp', 'mp')
- input_grad: bfloat16 [512, 8192], P('dp', 'mp')
- tile_grads: float32 [2, 1344, 128, 128], P(None, 'mp')
Inputs may be any that keep to these rules, and one draw needn't show every extreme that they name: `tile_rows`: row m lists the tiles of matrix m; device k // 168 of mp owns tile k. Within one column panel of one matrix the row blocks are distinct. `tile_cols`: A column panel holds 12 or 4 tiles, the same count for all 28 panels of one holder (panels c with equal c // 28), 12 for a quarter of the holders. An owner's tiles are listed in the order of their panels. At most 42 of one owner's tiles of a matrix lie in one holder's panels, and this bound is reached in every matrix.
All inputs are finite; a program needn't handle non-finite values.
Results may differ from a plain program's by a relative error of at most 0.02.
Values may be sent and summed in bfloat16 or wider, within the bound.
A program may use at most 192 MiB of HBM per device.

v0:
```python
import jax
import jax.numpy as jnp
from jax import lax
from jax.sharding import PartitionSpec as P

KHEAVY = 12


def per_device(tokens, cotangent, tiles, tile_rows, tile_cols):
    members = lax.axis_size("mp")
    myself = lax.axis_index("mp")
    tile_size = tiles.shape[-1]
    owned_count = tiles.shape[1]
    tok_rows = tokens.shape[0]
    feature_width = tokens.shape[1] * members
    row_blocks = feature_width // tile_size
    panels = cotangent.shape[1] // tile_size
    capacity = (panels * KHEAVY + members - 1) // members
    slot_count = members * capacity
    rows_all = tile_rows.reshape(2, members, owned_count)
    cols_all = tile_cols.reshape(2, members, owned_count)
    holder_all = cols_all // panels
    earlier = jnp.arange(owned_count)[:, None] > jnp.arange(owned_count)[None, :]
    same_holder = holder_all[:, :, :, None] == holder_all[:, :, None, :]
    rank_all = jnp.sum((same_holder & earlier).astype(jnp.int32), axis=3)
    my_holder = lax.dynamic_index_in_dim(holder_all, myself, 1, keepdims=False)
    my_rank = lax.dynamic_index_in_dim(rank_all, myself, 1, keepdims=False)
    slot_ids = my_holder * capacity + my_rank
    matrices = jnp.arange(2)[:, None]
    outgoing = (
        jnp.zeros((2, slot_count, tile_size, tile_size), jnp.bfloat16)
        .at[matrices, slot_ids]
        .set(tiles)
    )
    incoming = lax.all_to_all(
        outgoing.reshape(2, members, capacity, tile_size, tile_size),
        "mp",
        split_axis=1,
        concat_axis=1,
        tiled=True,
    )
    incoming = incoming.reshape(2 * slot_count, tile_size, tile_size)
    matches = (holder_all[:, :, None, :] == myself) & (
        rank_all[:, :, None, :] == jnp.arange(capacity)[None, None, :, None]
    )
    slot_rows = jnp.sum(jnp.where(matches, rows_all[:, :, None, :], 0), axis=3).reshape(
        2, slot_count
    )
    slot_cols = jnp.sum(
        jnp.where(matches, cols_all[:, :, None, :] - myself * panels, 0), axis=3
    ).reshape(2, slot_count)
    all_rows = slot_rows.reshape(-1)
    all_cols = (slot_cols + matrices * panels).reshape(-1)
    gathered = lax.all_gather(tokens, "mp", axis=1, tiled=True)
    grouped = jnp.transpose(gathered.reshape(tok_rows, row_blocks, tile_size), (1, 0, 2))
    picked = jnp.take(grouped, all_rows, axis=0)
    partial_value = jnp.einsum("sni,sij->snj", picked, incoming, preferred_element_type=jnp.float32)
    summed = jax.ops.segment_sum(partial_value, all_cols, num_segments=2 * panels)
    summed = jnp.transpose(summed.reshape(2, panels, tok_rows, tile_size), (0, 2, 1, 3)).reshape(
        2, tok_rows, panels * tile_size
    )
    gate_pre = summed[0]
    up_pre = summed[1]
    sigmoid_gate = jax.nn.sigmoid(gate_pre)
    hidden = (gate_pre * sigmoid_gate * up_pre).astype(jnp.bfloat16)
    upstream = cotangent.astype(jnp.float32)
    gate_grad = (upstream * up_pre * sigmoid_gate * (1.0 + gate_pre * (1.0 - sigmoid_gate))).astype(
        jnp.bfloat16
    )
    up_grad = (upstream * gate_pre * sigmoid_gate).astype(jnp.bfloat16)
    grad_panels = jnp.transpose(
        jnp.stack([gate_grad, up_grad]).reshape(2, tok_rows, panels, tile_size), (0, 2, 1, 3)
    )
    grad_panels = grad_panels.reshape(2 * panels, tok_rows, tile_size)
    columns = jnp.take(grad_panels, all_cols, axis=0)
    grads_slot = jnp.einsum(
        "sni,snj->sij", picked, columns, preferred_element_type=jnp.float32
    ).astype(jnp.bfloat16)
    back_terms = jnp.einsum("snj,sij->sni", columns, incoming, preferred_element_type=jnp.float32)
    input_terms = jax.ops.segment_sum(back_terms, all_rows, num_segments=row_blocks)
    stacked = grads_slot.reshape(2, members, capacity, tile_size, tile_size)
    returned = lax.all_to_all(stacked, "mp", split_axis=1, concat_axis=1, tiled=True).reshape(
        2, slot_count, tile_size, tile_size
    )
    own_grads = returned[matrices, slot_ids]
    input_terms = jnp.transpose(input_terms, (1, 0, 2)).reshape(tok_rows, feature_width)
    input_grad = lax.psum_scatter(
        input_terms.astype(jnp.bfloat16), "mp", scatter_dimension=1, tiled=True
    )
    tile_grads = lax.psum(own_grads.astype(jnp.float32).astype(jnp.bfloat16), "dp").astype(
        jnp.float32
    )
    return (hidden, input_grad, tile_grads)


def solution(mesh):
    in_specs = (P("dp", "mp"), P("dp", "mp"), P(None, "mp", None, None), P(), P())
    out_specs = (P("dp", "mp"), P("dp", "mp"), P(None, "mp", None, None))
    return jax.shard_map(
        per_device, mesh=mesh, in_specs=in_specs, out_specs=out_specs, check_vma=False
    )
```

profile of v0, /device:TPU:0, one launch (start us, length us, event | category | flops | bytes accessed | tf_op | source)
XLA Modules:
  0.0 1630.9 jit_solution(4399142335656311216)
XLA Ops:
  7.2 0.7 compare_and_fusion
  8.0 0.7 broadcast_subtract_fusion
  8.7 0.1 div.24
  8.8 0.1 and.50
  8.9 1.2 convert_reduce_fusion
  10.1 0.6 fusion.21
  10.7 0.1 reshape.274
  10.8 8.0 broadcast_in_dim.73
  18.7 53.5 %scatter_fusion = bf16[2,336,128,128]{3,2,1,0:T(8,128)(2,1)} fusion(bf16[2,336,128,128]{3,2,1,0:T(8,128)(2,1)} %broadcast_in_dim.73, s32[336]{0:T(512)S(1)} %reshape.274, bf16[336,128,128]{2,1,0:T(8,128)(2,1)} %bitcast.60), kind=kCustom, calls=%fused_computation.3 | custom fusion | bytes 33032832 | tf_op jit(solution)/shard_map/scatter | solution.py:33
  72.3 19.0 %copy.72 = bf16[2,8,42,128,128]{4,3,2,0,1:T(8,128)(2,1)} copy(bf16[2,8,42,128,128]{4,3,2,1,0:T(8,128)(2,1)} %bitcast.56) | data formatting | bytes 44040192 | tf_op jit(solution)/shard_map/reshape | solution.py:36
  91.2 7.4 all-to-all-start
  98.6 0.0 all-gather.2.cloned.1.call-start
  98.7 0.8 copy.69
  99.5 0.0 all-gather.2.cloned.1.call-update
  99.6 0.1 sub.26
  99.7 0.1 broadcast_in_dim.69
  99.8 2.9 select_reduce_fusion
  102.7 0.1 copy.68
  102.7 0.1 reshape_reshape.5
  102.8 0.1 reshape_reshape.6
  102.9 0.1 copy.67
  103.0 0.1 reshape.248
  103.1 0.1 reshape.243
  103.2 0.1 add.129
  103.3 0.1 add.141
  103.4 0.1 add.130
  103.4 0.8 copy.77
  104.3 387.6 %all-gather.2.cloned.1.call-done = bf16[128,8192]{0,1:T(8,128)(2,1)} async-done(((bf16[128,1024]{0,1:T(8,128)(2,1)}), bf16[128,8192]{0,1:T(8,128)(2,1)}) %all-gather.2.cloned.1.call-update) | async-done | bytes 2097168 | tf_op jit(solution)/shard_map/all_gather | solution.py:54
  491.9 3.2 copy.70
  495.1 17.3 %gather_fusion = bf16[672,128,128]{2,1,0:T(8,128)(2,1)} fusion(bf16[64,128,128]{2,1,0:T(8,128)(2,1)S(1)} %bitcast.53, s32[1024]{0:T(1024)S(1)} %pad_clamp_fusion.1), kind=kCustom, calls=%fused_computation | custom fusion | bytes 44042880 | tf_op jit(solution)/shard_map/jit(_take)/gather | solution.py:56
  512.4 87.3 %all-to-all-done = bf16[2,8,42,128,128]{4,3,2,0,1:T(8,128)(2,1)} async-done(((bf16[2,8,42,128,128]{4,3,2,0,1:T(8,128)(2,1)}), bf16[2,8,42,128,128]{4,3,2,0,1:T(8,128)(2,1)}, u32[]{:S(2)}, u32[]{:S(2)}) %all-to-all-start) | async-done | bytes 22020128 | tf_op jit(solution)/shard_map/all_to_all | solution.py:35
  599.8 18.9 %copy.73 = bf16[2,8,42,128,128]{4,3,2,1,0:T(8,128)(2,1)} copy(bf16[2,8,42,128,128]{4,3,2,0,1:T(8,128)(2,1)} %all-to-all-done) | data formatting | bytes 44040192 | tf_op jit(solution)/shard_map/all_to_all | solution.py:35
  618.7 28.5 %fusion = f32[672,128,128]{2,1,0:T(8,128)} fusion(bf16[672,128,128]{2,1,0:T(8,128)(2,1)} %bitcast.54, bf16[672,128,128]{2,1,0:T(8,128)(2,1)} %gather_fusion, pred[672]{0:T(1024)(128)(4,1)S(1)} %get-tuple-element.37), kind=kOutput, calls=%fused_computation.9 | convolution fusion | flops 2829582336 | bytes 88081056 | tf_op jit(solution)/shard_map/sni,sij->snj/dot_general | solution.py:57
  647.2 2.3 broadcast_in_dim.66
  649.5 147.2 %scatter_fusion.1 = f32[56,128,128]{2,1,0:T(8,128)} fusion(f32[56,128,128]{2,1,0:T(8,128)} %broadcast_in_dim.66, s32[672]{0:T(1024)S(1)} %get-tuple-element.24, f32[672,128,128]{2,1,0:T(8,128)} %fusion), kind=kCustom, calls=%fused_computation.4 | custom fusion | flops 11010048 | bytes 132123264 | tf_op jit(solution)/shard_map/scatter-add | solution.py:58
  796.6 4.3 fusion.22
  800.9 1.8 copy.74
  802.7 2.7 copy.75
  805.5 3.5 fusion.4
  809.0 1.4 maximum_bitcast_fusion
  810.4 2.9 copy.78
  813.3 17.5 %gather_fusion.1 = bf16[672,128,128]{2,1,0:T(8,128)(2,1)} fusion(bf16[56,128,128]{2,1,0:T(8,128)(2,1)S(1)} %bitcast.52, s32[1024]{0:T(1024)S(1)} %pad_clamp_fusion), kind=kCustom, calls=%fused_computation.1 | custom fusion | bytes 44042880 | tf_op jit(solution)/shard_map/jit(_take)/gather | solution.py:75
  830.8 23.5 %convolution_convert_fusion = bf16[672,128,128]{2,1,0:T(8,128)(2,1)} fusion(bf16[672,128,128]{2,1,0:T(8,128)(2,1)} %gather_fusion, pred[672]{0:T(1024)(128)(4,1)S(1)} %get-tuple-element.37, bf16[672,128,128]{2,1,0:T(8,128)(2,1)} %gather_fusion.1, pred[672]{0:T(1024)(128)(4,1)S(1)} %get-tuple-element.36), kind=kOutput, calls=%fused_computation.8 | convolution fusion | flops 2851602432 | bytes 66061632 | tf_op jit(solution)/shard_map/sni,snj->sij/dot_general | solution.py:76
  854.3 18.9 %copy.81 = bf16[2,8,42,128,128]{4,3,2,0,1:T(8,128)(2,1)} copy(bf16[2,8,42,128,128]{4,3,2,1,0:T(8,128)(2,1)} %bitcast.59) | data formatting | bytes 44040192 | tf_op jit(solution)/shard_map/reshape | solution.py:81
  873.3 6.2 all-to-all-start.1
  879.5 0.0 reduce-scatter.2.cloned.1.call-start
  879.5 31.9 %fusion.1 = f32[672,128,128]{2,1,0:T(8,128)} fusion(bf16[672,128,128]{2,1,0:T(8,128)(2,1)} %bitcast.55, bf16[672,128,128]{2,1,0:T(8,128)(2,1)} %gather_fusion.1, pred[672]{0:T(1024)(128)(4,1)S(1)} %get-tuple-element.36), kind=kOutput, calls=%fused_computation.10 | convolution fusion | flops 2829582336 | bytes 88081056 | tf_op jit(solution)/shard_map/snj,sij->sni/dot_general | solution.py:79
  911.4 2.5 broadcast_in_dim.75
  914.0 141.1 %scatter_fusion.2 = f32[64,128,128]{2,1,0:T(8,128)} fusion(f32[64,128,128]{2,1,0:T(8,128)} %broadcast_in_dim.75, s32[672]{0:T(1024)S(1)} %copy-done.4, f32[672,128,128]{2,1,0:T(8,128)} %fusion.1), kind=kCustom, calls=%fused_computation.5 | custom fusion | flops 11010048 | bytes 132123264 | tf_op jit(solution)/shard_map/scatter-add | solution.py:80
  1055.0 2.6 convert_bitcast_fusion
  1057.6 2.9 copy.79
  1060.5 0.0 reduce-scatter.2.cloned.1.call-update
  1060.6 0.0 all-reduce.2.cloned.1.call-start
  1060.6 0.1 reshape.268
  1060.7 310.6 %all-to-all-done.1 = bf16[2,8,42,128,128]{4,3,2,0,1:T(8,128)(2,1)} async-done(((bf16[2,8,42,128,128]{4,3,2,0,1:T(8,128)(2,1)}), bf16[2,8,42,128,128]{4,3,2,0,1:T(8,128)(2,1)}, u32[]{:S(2)}, u32[]{:S(2)}) %all-to-all-start.1) | async-done | bytes 22020128 | tf_op jit(solution)/shard_map/all_to_all | solution.py:82
  1371.3 19.0 %copy.82 = bf16[2,8,42,128,128]{4,3,2,1,0:T(8,128)(2,1)} copy(bf16[2,8,42,128,128]{4,3,2,0,1:T(8,128)(2,1)} %all-to-all-done.1) | data formatting | bytes 44040192 | tf_op jit(solution)/shard_map/all_to_all | solution.py:82
  1390.3 27.2 %gather_fusion.2 = bf16[336,128,128]{2,1,0:T(8,128)(2,1)} fusion(bf16[2,336,128,128]{3,2,1,0:T(8,128)(2,1)} %bitcast.57, s32[336]{0:T(512)S(1)} %reshape.268), kind=kCustom, calls=%fused_computation.2 | custom fusion | bytes 22022784 | tf_op jit(solution)/shard_map/gather | solution.py:85
  1417.6 0.0 copy-start
  1417.6 0.0 all-reduce.2.cloned.1.call-update
  1417.6 1.1 copy-done
  1418.7 1.3 copy.83
  1420.0 1.8 copy.84
  1421.8 190.0 %all-reduce.2.cloned.1.call-done = bf16[2,168,128,128]{3,2,1,0:T(8,128)(2,1)} async-done(((bf16[2,168,128,128]{3,2,1,0:T(8,128)(2,1)}), bf16[2,168,128,128]{3,2,1,0:T(8,128)(2,1)}) %all-reduce.2.cloned.1.call-update) | async-done | bytes 11010064 | tf_op jit(solution)/shard_map/psum | solution.py:90
  1611.8 12.6 convert_element_type.41
  (21 shorter events, 0.1 us)
Async XLA Ops:
  91.2 7.4 copy-start.2
  91.2 8.4 copy-start.5
  91.2 12.2 copy-start.1
  91.2 508.5 %all-to-all-start = ((bf16[2,8,42,128,128]{4,3,2,0,1:T(8,128)(2,1)}), bf16[2,8,42,128,128]{4,3,2,0,1:T(8,128)(2,1)}, u32[]{:S(2)}, u32[]{:S(2)}) async-start(bf16[2,8,42,128,128]{4,3,2,0,1:T(8,128)(2,1)} %copy.72), calls=%async_computation | async-start | bytes 44040192 | tf_op jit(solution)/shard_map/all_to_all | solution.py:35
  98.6 393.3 %all-gather.2.cloned.1.call-start = ((), (), s32[]{:S(2)}) async-start(), calls=%async_computation.3 | async-start | bytes 2359296 | tf_op jit(solution)/shard_map/all_gather | solution.py:54
  102.8 389.1 %copy-start.3 = (s32[672]{0:T(1024)}, s32[672]{0:T(1024)S(1)}, u32[]{:S(2)}) copy-start(s32[672]{0:T(1024)S(1)} %reshape_reshape.5) | copy-start | bytes 8068
  873.3 498.1 %all-to-all-start.1 = ((bf16[2,8,42,128,128]{4,3,2,0,1:T(8,128)(2,1)}), bf16[2,8,42,128,128]{4,3,2,0,1:T(8,128)(2,1)}, u32[]{:S(2)}, u32[]{:S(2)}) async-start(bf16[2,8,42,128,128]{4,3,2,0,1:T(8,128)(2,1)} %copy.81), calls=%async_computation.2 | async-start | bytes 44040192 | tf_op jit(solution)/shard_map/all_to_all | solution.py:82
  879.5 34.5 %copy-start.4 = (s32[672]{0:T(1024)S(1)}, s32[672]{0:T(1024)}, u32[]{:S(2)}) copy-start(s32[672]{0:T(1024)} %copy-done.3) | copy-start | bytes 8068
  879.5 540.5 %reduce-scatter.2.cloned.1.call-start = ((), (), s32[]{:S(2)}) async-start(), calls=%async_computation.4 | async-start | bytes 2359296 | tf_op jit(solution)/shard_map/reduce_scatter | solution.py:87
  1055.0 5.6 copy-start.6
  1060.6 551.2 %all-reduce.2.cloned.1.call-start = ((), (), s32[]{:S(2)}) async-start(), calls=%async_computation.5 | async-start | bytes 22020096 | tf_op jit(solution)/shard_map/psum | solution.py:90
  1417.6 1.2 copy-start
Sparse Core Ops, SparseCore 0:
  102.2 389.6 all-gather.1
  1060.7 343.7 reduce-scatter.1
  1417.7 194.0 all-reduce.1
where the time goes:
time: 1640 us; the launch traced here: 1630 us
  waiting for transfers between devices  976 us (60%)
  other arithmetic  315 us (19%)
  local copies, waits for them, and re-layouts  229 us (14%)
  matrix products  83.9 us (5%)
    all_gather x1, waiting for transfers between devices, per_device(): gathered = lax.all_gather(tokens, 'mp', axis=1, tiled=True)  388 us
    all_to_all x1, waiting for transfers between devices, per_device(): lax.all_to_all(stacked, 'mp', split_axis=1, concat_axis=1, tiled=True)  311 us
    psum x1, waiting for transfers between devices, per_device(): lax.psum(own_grads.astype(jnp.float32).astype(jnp.bfloat16), 'dp')  190 us
    scatter-add x1, other arithmetic, per_device(): jax.ops.segment_sum(partial_value, all_cols, num_segments=2 * panels)  147 us
    scatter-add x1, other arithmetic, per_device(): jax.ops.segment_sum(back_terms, all_rows, num_segments=row_blocks)  141 us
    all_to_all x1, waiting for transfers between devices, per_device(): lax.all_to_all(outgoing.reshape(2, members, capacity, tile_size, tile_siz...  87.3 us
    scatter x1, local copies, waits for them, and re-layouts, per_device(): outgoing = jnp.zeros((2, slot_count, tile_size, tile_size), jnp.bfloat16)...  53.5 us
  transfers between devices with their start and end apart: 5, of which 4 were waited for; matrix products, arithmetic and copies ran while one was open for 16% of the time, Pallas kernels for 0%

commit v1 on v0

v1 whole, which is shorter than its diff:
```python
import jax
import jax.numpy as jnp
from jax import lax
from jax.experimental import pallas as pl
from jax.experimental.pallas import tpu as pltpu
from jax.sharding import PartitionSpec as P

KHEAVY = 12
KLIGHT = 4
CORES = 2
VMEM_BYTES = 50 * 1024 * 1024


def load_halves(first_ref, second_ref, buf, sems):
    half = first_ref.shape[0]
    copies = [
        pltpu.make_async_copy(first_ref, buf.at[pl.ds(0, half)], sems.at[0]),
        pltpu.make_async_copy(second_ref, buf.at[pl.ds(half, half)], sems.at[1]),
    ]
    for copy in copies:
        copy.start()
    for copy in copies:
        copy.wait()


def forward_kernel(slots, rows, steps, tok_ref, first_ref, second_ref, pre_ref, buf, sems):
    load_halves(first_ref, second_ref, buf, sems)
    size = tok_ref.shape[-1]
    panels = pre_ref.shape[1] // size

    def panel_step(p, carry):
        def group(t, total):
            base = p * KHEAVY + t * KLIGHT
            left = jnp.concatenate([tok_ref[rows[base + i]] for i in range(KLIGHT)], axis=1)
            right = jnp.concatenate([buf[slots[base + i]] for i in range(KLIGHT)], axis=0)
            return total + jnp.dot(left, right, preferred_element_type=jnp.float32)

        total = lax.fori_loop(0, steps[0], group, jnp.zeros((tok_ref.shape[1], size), jnp.float32))
        pre_ref[:, pl.ds(pl.multiple_of(p * size, size), size)] = total
        return carry

    lax.fori_loop(0, panels, panel_step, 0)


def backward_kernel(
    slots, rows, steps, tokt_ref, grad_ref, first_ref, second_ref,
    terms_ref, out_first, out_second, buf, grads, sems
):
    load_halves(first_ref, second_ref, buf, sems)
    size = tokt_ref.shape[1]
    panels = grad_ref.shape[1] // size
    terms_ref[...] = jnp.zeros_like(terms_ref)

    def panel_step(p, carry):
        column = grad_ref[:, pl.ds(pl.multiple_of(p * size, size), size)]

        def group(t, inner):
            base = p * KHEAVY + t * KLIGHT
            row = [rows[base + i] for i in range(KLIGHT)]
            slot = [slots[base + i] for i in range(KLIGHT)]
            weight = jnp.concatenate([buf[s] for s in slot], axis=0)
            back = lax.dot_general(
                column, weight, (((1,), (1,)), ((), ())), preferred_element_type=jnp.float32
            )
            picked = jnp.concatenate([tokt_ref[r] for r in row], axis=0)
            outer = jnp.dot(picked, column, preferred_element_type=jnp.float32).astype(grads.dtype)
            before = [terms_ref[r] for r in row]
            for i in range(KLIGHT):
                terms_ref[row[i]] = before[i] + back[:, i * size : (i + 1) * size]
                grads[slot[i]] = outer[i * size : (i + 1) * size]
            return inner

        return lax.fori_loop(0, steps[0], group, carry)

    lax.fori_loop(0, panels, panel_step, 0)
    half = out_first.shape[0]
    copies = [
        pltpu.make_async_copy(grads.at[pl.ds(0, half)], out_first, sems.at[0]),
        pltpu.make_async_copy(grads.at[pl.ds(half, half)], out_second, sems.at[1]),
    ]
    for copy in copies:
        copy.start()
    for copy in copies:
        copy.wait()


def collect_kernel(slots, g_first, g_second, u_first, u_second, out_ref, buf, sems):
    m, c = pl.program_id(0), pl.program_id(1)

    @pl.when((m == 0) & (c == 0))
    def _():
        load_halves(g_first, g_second, buf, sems)

    @pl.when((m == 1) & (c == 0))
    def _():
        load_halves(u_first, u_second, buf, sems)

    chunk = out_ref.shape[1]
    owned = chunk * pl.num_programs(1)

    def step(i, carry):
        out_ref[0, i] = buf[slots[m * owned + c * chunk + i]].astype(jnp.float32)
        return carry

    lax.fori_loop(0, chunk, step, 0)


def per_device(tokens, cotangent, tiles, tile_rows, tile_cols):
    members = lax.axis_size("mp")
    myself = lax.axis_index("mp")
    groups = lax.axis_size("dp")
    group_id = lax.axis_index("dp")
    lanes = groups // CORES
    my_y, my_core = group_id // CORES, group_id % CORES
    size = tiles.shape[-1]
    owned = tiles.shape[1]
    tok_rows = tokens.shape[0]
    local_blocks = tokens.shape[1] // size
    row_blocks = local_blocks * members
    panels = cotangent.shape[1] // size
    capacity = (panels * KHEAVY + members - 1) // members
    share = (capacity + groups - 1) // groups
    quarter = members * share
    half = lanes * quarter
    smem = pl.BlockSpec(memory_space=pltpu.SMEM)
    vmem = pl.BlockSpec(memory_space=pltpu.VMEM)
    anywhere = pl.BlockSpec(memory_space=pl.ANY)

    def place(rank, partner):
        sender = rank % groups
        core_off = (sender % CORES + my_core) % CORES
        y_off = (my_y - sender // CORES + lanes) % lanes
        return core_off * half + y_off * quarter + partner * share + rank // groups

    def swap_cores(x):
        pairs = [(d, d - 1 if d % CORES else d + 1) for d in range(groups)]
        return lax.ppermute(x, "dp", pairs)

    def shift_y(x, by):
        pairs = [
            (d, ((d // CORES + by) % lanes) * CORES + d % CORES) for d in range(groups)
        ]
        return lax.ppermute(x, "dp", pairs)

    def spread(x):
        stacked = jnp.concatenate([x] + [shift_y(x, s) for s in range(1, lanes)], axis=0)
        return stacked, swap_cores(stacked)

    def exchange(x):
        swapped = lax.all_to_all(
            x.reshape(members, share, size, size), "mp", split_axis=0, concat_axis=0, tiled=True
        )
        return swapped.reshape(quarter, size, size)

    cols_all = tile_cols.reshape(2, members, owned)
    holder_all = cols_all // panels
    my_holder = lax.dynamic_index_in_dim(holder_all, myself, 1, keepdims=False)
    member_ids = jnp.arange(members, dtype=jnp.int32)
    tile_ids = jnp.arange(owned, dtype=jnp.int32)
    start = jnp.sum(
        (my_holder[:, None, :] < member_ids[None, :, None]).astype(jnp.int32), axis=2
    )
    source = (
        start[:, :, None] + jnp.arange(share, dtype=jnp.int32)[None, None, :] * groups + group_id
    )
    source = jnp.minimum(source, owned - 1) + jnp.arange(2, dtype=jnp.int32)[:, None, None] * owned
    flat_tiles = tiles.reshape(2 * owned, size, size)
    arrived = [
        spread(exchange(jnp.take(flat_tiles, source[m].reshape(-1), axis=0, mode="clip")))
        for m in range(2)
    ]

    blocks = jnp.transpose(tokens.reshape(tok_rows, local_blocks, size), (1, 0, 2))
    tok = lax.all_gather(blocks, "mp", axis=0, tiled=True)
    tokt = jnp.transpose(tok, (0, 2, 1))

    first = jnp.sum((holder_all < myself).astype(jnp.int32), axis=2)
    slot_all = place(
        jnp.maximum(tile_ids[None, None, :] - first[:, :, None], 0), member_ids[None, :, None]
    ).reshape(2, -1)
    local_cols = tile_cols - myself * panels
    mask = local_cols[:, None, :] == jnp.arange(panels, dtype=jnp.int32)[None, :, None]
    listed = jnp.arange(tile_cols.shape[1])
    before = (listed[:, None] < listed[None, :]).astype(jnp.bfloat16)
    rank = jnp.einsum(
        "mpk,kl->mpl", mask.astype(jnp.bfloat16), before, preferred_element_type=jnp.float32
    ).astype(jnp.int32)
    chosen = mask[:, :, None, :] & (
        rank[:, :, None, :] == jnp.arange(KHEAVY, dtype=jnp.int32)[None, None, :, None]
    )
    slots = jnp.sum(jnp.where(chosen, slot_all[:, None, None, :], 0), axis=3).reshape(2, -1)
    rows = jnp.sum(jnp.where(chosen, tile_rows[:, None, None, :], 0), axis=3).reshape(2, -1)
    steps = jnp.sum(mask[:, 0, :].astype(jnp.int32), axis=1) // KLIGHT

    slot_bytes = 2 * half * size * size * 2
    flops = 2 * panels * KHEAVY * size**2 * tok_rows
    tile_buf = pltpu.VMEM((2 * half, size, size), jnp.bfloat16)
    params = pltpu.CompilerParams(vmem_limit_bytes=VMEM_BYTES)

    def project(m):
        return pl.pallas_call(
            forward_kernel,
            out_shape=jax.ShapeDtypeStruct(cotangent.shape, jnp.float32),
            in_specs=[smem, smem, smem, vmem, anywhere, anywhere],
            out_specs=vmem,
            scratch_shapes=[tile_buf, pltpu.SemaphoreType.DMA((2,))],
            compiler_params=params,
            cost_estimate=pl.CostEstimate(
                flops=flops, bytes_accessed=4 * slot_bytes, transcendentals=0
            ),
            name="project",
        )(slots[m], rows[m], steps[m : m + 1], tok, *arrived[m])

    gate_pre, up_pre = project(0), project(1)
    sigmoid_gate = jax.nn.sigmoid(gate_pre)
    hidden = (gate_pre * sigmoid_gate * up_pre).astype(jnp.bfloat16)
    upstream = cotangent.astype(jnp.float32)
    gate_grad = (upstream * up_pre * sigmoid_gate * (1.0 + gate_pre * (1.0 - sigmoid_gate))).astype(
        jnp.bfloat16
    )
    up_grad = (upstream * gate_pre * sigmoid_gate).astype(jnp.bfloat16)

    def pull_back(m, grad):
        half_shape = jax.ShapeDtypeStruct((half, size, size), jnp.bfloat16)
        return pl.pallas_call(
            backward_kernel,
            out_shape=(
                jax.ShapeDtypeStruct((row_blocks, tok_rows, size), jnp.float32),
                half_shape,
                half_shape,
            ),
            in_specs=[smem, smem, smem, vmem, vmem, anywhere, anywhere],
            out_specs=(vmem, anywhere, anywhere),
            scratch_shapes=[tile_buf, tile_buf, pltpu.SemaphoreType.DMA((2,))],
            compiler_params=params,
            cost_estimate=pl.CostEstimate(
                flops=2 * flops, bytes_accessed=6 * slot_bytes, transcendentals=0
            ),
            name="pull_back",
        )(slots[m], rows[m], steps[m : m + 1], tokt, grad, *arrived[m])

    def total_of(kept, sent):
        wide = kept.astype(jnp.float32) + swap_cores(sent).astype(jnp.float32)
        pair = wide.astype(jnp.bfloat16).reshape(lanes, quarter, size, size)
        total = pair[0].astype(jnp.float32)
        for s in range(1, lanes):
            total = total + shift_y(pair[s], lanes - s).astype(jnp.float32)
        return spread(exchange(total.astype(jnp.bfloat16)))

    gate_terms, gate_kept, gate_sent = pull_back(0, gate_grad)
    gate_home = total_of(gate_kept, gate_sent)
    up_terms, up_kept, up_sent = pull_back(1, up_grad)
    up_home = total_of(up_kept, up_sent)

    terms = (gate_terms + up_terms).astype(jnp.bfloat16)
    mine = lax.psum_scatter(terms, "mp", scatter_dimension=0, tiled=True)
    input_grad = jnp.transpose(mine, (1, 0, 2)).reshape(tokens.shape)

    my_start = jnp.sum(
        (my_holder[:, None, :] < my_holder[:, :, None]).astype(jnp.int32), axis=2
    )
    home = place(tile_ids[None, :] - my_start, my_holder).reshape(-1)
    chunk = max(c for c in range(1, 29) if owned % c == 0)
    tile_grads = pl.pallas_call(
        collect_kernel,
        out_shape=jax.ShapeDtypeStruct(tiles.shape, jnp.float32),
        grid=(2, owned // chunk),
        in_specs=[smem, anywhere, anywhere, anywhere, anywhere],
        out_specs=pl.BlockSpec((1, chunk, size, size), lambda m, c: (m, c, 0, 0)),
        scratch_shapes=[tile_buf, pltpu.SemaphoreType.DMA((2,))],
        compiler_params=params,
        name="collect",
    )(home, *gate_home, *up_home)
    return (hidden, input_grad, tile_grads)


def solution(mesh):
    in_specs = (P("dp", "mp"), P("dp", "mp"), P(None, "mp", None, None), P(), P())
    out_specs = (P("dp", "mp"), P("dp", "mp"), P(None, "mp", None, None))
    return jax.shard_map(
        per_device, mesh=mesh, in_specs=in_specs, out_specs=out_specs, check_vma=False
    )
```

time: 1640 us -> 757 us (0.46)
  waiting for transfers between devices: 976 us -> 523 us
  other arithmetic: 315 us -> 57.3 us
  local copies, waits for them, and re-layouts: 229 us -> 28.2 us
  Pallas kernels: 0 us -> 102 us
  matrix products: 83.9 us -> 0.61 us
  starting transfers between devices: 13.7 us -> 31.1 us
    all_gather x1, waiting for transfers between devices: 388 us -> 33.6 us  [per_device(): tok = lax.all_gather(blocks, 'mp', axis=0, tiled=True)]
    scatter-add x2 -> x0, other arithmetic: 288 us -> none  [the longest x1 147 us: per_device(): jax.ops.segment_sum(partial_value, all_cols, num_segments=2 * panels)]
    ppermute x0 -> x12, waiting for transfers between devices: none -> 237 us  [the longest x6 237 us: shift_y(): return lax.ppermute(x, 'dp', pairs)]
    all_to_all x2 -> x4, waiting for transfers between devices: 398 us -> 183 us  [exchange(): lax.all_to_all(x.reshape(members, share, size, size), 'mp', split_axis=0,...]
    psum x1 -> x0, waiting for transfers between devices: 190 us -> none  [per_device(): lax.psum(own_grads.astype(jnp.float32).astype(jnp.bfloat16), 'dp')]
    pallas_call x0 -> x5, Pallas kernels: none -> 102 us  [the longest x2 50.7 us: pull_back(): pl.pallas_call(backward_kernel, out_shape=(jax.ShapeDtypeStruct((row_bloc...]
    dot_general x3 -> x1, matrix products: 83.9 us -> 0.61 us  [per_device(): jnp.einsum('mpk,kl->mpl', mask.astype(jnp.bfloat16), before, preferred_el...]
    reduce_scatter x1, waiting for transfers between devices: 0.01 us -> 69.6 us  [per_device(): mine = lax.psum_scatter(terms, 'mp', scatter_dimension=0, tiled=True)]
  transfers between devices with their start and end apart: 5 -> 18, of which waited for: 4 -> 9; matrix products, arithmetic and copies ran while one was open for 16% -> 10% of each run, Pallas kernels for 0% -> 4%
where the time goes in v1:
time: 757 us; the launch traced here: 756 us
  waiting for transfers between devices  523 us (69%)
  Pallas kernels  102 us (13%)
  other arithmetic  57.3 us (8%)
  starting transfers between devices  31.1 us (4%)
  local copies, waits for them, and re-layouts  28.2 us (4%)
  between operations  14.4 us (2%)
    ppermute x6, waiting for transfers between devices, shift_y(): return lax.ppermute(x, 'dp', pairs)  237 us
    all_to_all x4, waiting for transfers between devices, exchange(): lax.all_to_all(x.reshape(members, share, size, size), 'mp', split_axis=0,...  183 us
    reduce_scatter x1, waiting for transfers between devices, per_device(): mine = lax.psum_scatter(terms, 'mp', scatter_dimension=0, tiled=True)  69.6 us
    pallas_call x2, Pallas kernels, pull_back(): pl.pallas_call(backward_kernel, out_shape=(jax.ShapeDtypeStruct((row_bloc...  50.7 us
    all_gather x1, waiting for transfers between devices, per_device(): tok = lax.all_gather(blocks, 'mp', axis=0, tiled=True)  33.6 us
    pallas_call x2, Pallas kernels, project(): pl.pallas_call(forward_kernel, out_shape=jax.ShapeDtypeStruct(cotangent.s...  31.9 us
    all_to_all x4, starting transfers between devices, exchange(): lax.all_to_all(x.reshape(members, share, size, size), 'mp', split_axis=0,...  21.2 us
    pallas_call x1, Pallas kernels, per_device(): pl.pallas_call(collect_kernel, out_shape=jax.ShapeDtypeStruct(tiles.shape...  19.4 us
  transfers between devices with their start and end apart: 18, of which 9 were waited for; matrix products, arithmetic and copies ran while one was open for 10% of the time, Pallas kernels for 4%

profile of v1, /device:TPU:0, one launch (start us, length us, event | category | flops | bytes accessed | tf_op | source)
XLA Modules:
  0.0 756.5 jit_solution(3825683890677727049)
XLA Ops:
  7.2 0.7 compare_and_fusion.1
  7.9 0.1 and.138
  8.0 0.7 broadcast_divide_fusion
  8.9 0.1 convert_reduce_fusion.2
  9.1 0.1 convert_reduce_fusion.1
  9.4 6.8 gather_fusion
  16.1 7.3 all-to-all-start
  23.5 6.8 gather_fusion.1
  30.2 58.3 %all-to-all-done = bf16[8,11,128,128]{3,2,1,0:T(8,128)(2,1)S(1)} async-done(((bf16[8,11,128,128]{3,2,1,0:T(8,128)(2,1)}), bf16[8,11,128,128]{3,2,1,0:T(8,128)(2,1)S(1)}, u32[]{:S(2)}, u32[]{:S(2)}) %all-to-all-start) | async-done | bytes 2883616 | tf_op jit(solution)/shard_map/all_to_all | solution.py:150
  88.5 4.4 all-to-all-start.1
  93.0 1.6 collective-permute-start
  94.5 63.0 %all-to-all-done.1 = bf16[8,11,128,128]{3,2,1,0:T(8,128)(2,1)} async-done(((bf16[8,11,128,128]{3,2,1,0:T(8,128)(2,1)}), bf16[8,11,128,128]{3,2,1,0:T(8,128)(2,1)}, u32[]{:S(2)}, u32[]{:S(2)}) %all-to-all-start.1) | async-done | bytes 2883616 | tf_op jit(solution)/shard_map/all_to_all | solution.py:150
  157.5 1.5 collective-permute-start.2
  159.0 4.8 pad_maximum_fusion.first_ref
  163.8 56.5 %collective-permute-done.2 = bf16[88,128,128]{2,1,0:T(8,128)(2,1)S(1)} collective-permute-done((bf16[88,128,128]{2,1,0:T(8,128)(2,1)}, bf16[88,128,128]{2,1,0:T(8,128)(2,1)S(1)}, u32[]{:S(2)}, u32[]{:S(2)}) %collective-permute-start.2) | collective-permute-done | bytes 2883616 | tf_op jit(solution)/shard_map/ppermute | solution.py:143
  220.3 4.8 pad_maximum_fusion.1.first_ref
  225.2 0.2 copy.26
  225.3 0.9 copy.27
  226.6 0.1 sub.100
  226.7 0.1 copy.24
  226.9 0.6 fusion.3
  227.5 0.2 copy.25
  227.8 0.1 fusion.15
  227.9 11.9 %select_reduce_fusion = (s32[2,28,12]{0,2,1:T(8,128)S(1)}, s32[2,28,12]{0,2,1:T(8,128)S(1)}) fusion(pred[2,28,1344]{2,0,1:T(4,128)(4,1)S(1)} %copy.24, s32[2,1344]{1,0:T(2,128)S(1)} %copy-done.7, s32[2,28,1344]{2,0,1:T(2,128)S(1)} %copy.25, s32[2,1344]{1,0:T(2,128)S(1)} %fusion.15), kind=kLoop, calls=%fused_computation.15 | loop fusion | flops 5417664 | bytes 403200 | tf_op jit(solution)/shard_map/reduce_sum | solution.py:192
  239.8 2.1 slice_reduce_fusion.2
  241.9 0.1 squeeze.11.rows
  242.0 0.1 squeeze.13.rows
  242.1 0.1 squeeze.12.slots
  242.2 0.1 squeeze.10.slots
  242.3 0.1 fusion.18
  242.4 0.7 fusion.34
  243.1 33.6 %all-gather.2.cloned.1.call-done.tok_ref = bf16[64,128,128]{2,1,0:T(8,128)(2,1)} async-done(((bf16[8,128,128]{2,1,0:T(8,128)(2,1)}), bf16[64,128,128]{2,1,0:T(8,128)(2,1)}) %all-gather.2.cloned.1.call-update) | async-done | bytes 2097168 | tf_op jit(solution)/shard_map/all_gather | solution.py:174
  276.7 4.2 copy.28
  280.9 10.9 %project.2 = f32[128,3584]{1,0:T(8,128)S(1)} custom-call(s32[336]{0:T(512)S(1)} %squeeze.10.slots, s32[336]{0:T(512)S(1)} %squeeze.11.rows, s32[1]{0:T(128)} %get-tuple-element.44.steps, bf16[64,128,128]{2,1,0:T(8,128)(2,1)S(1)} %copy-done, bf16[176,128,128]{2,1,0:T(8,128)(2,1)} %pad_maximum_fusion.first_ref, ...), custom_call_target="tpu_custom_call" | custom-call | flops 1409286144 | bytes 46137344 | tf_op jit(solution)/shard_map/project/pallas_call | solution.py:201
  291.9 21.0 %project.3 = f32[128,3584]{1,0:T(8,128)S(1)} custom-call(s32[336]{0:T(512)S(1)} %squeeze.12.slots, s32[336]{0:T(512)S(1)} %squeeze.13.rows, s32[1]{0:T(128)} %get-tuple-element.45.steps, bf16[64,128,128]{2,1,0:T(8,128)(2,1)S(1)} %copy-done, bf16[176,128,128]{2,1,0:T(8,128)(2,1)} %pad_maximum_fusion.1.first_ref, ...), custom_call_target="tpu_custom_call" | custom-call | flops 1409286144 | bytes 46137344 | tf_op jit(solution)/shard_map/project/pallas_call | solution.py:201
  312.9 2.0 fusion.8
  314.9 31.7 %pull_back.3 = (f32[64,128,128]{2,1,0:T(8,128)}, bf16[176,128,128]{2,1,0:T(8,128)(2,1)}, bf16[176,128,128]{2,1,0:T(8,128)(2,1)}) custom-call(s32[336]{0:T(512)S(1)} %squeeze.12.slots, s32[336]{0:T(512)S(1)} %squeeze.13.rows, s32[1]{0:T(128)} %get-tuple-element.45.steps, bf16[64,128,128]{2,1,0:T(8,128)(2,1)S(1)} %bitcast.23, ...), custom_call_target="tpu_custom_call" | custom-call | flops 2818572288 | bytes 69206016 | tf_op jit(solution)/shard_map/pull_back/pallas_call | solution.py:225
  346.7 19.0 %pull_back.2 = (f32[64,128,128]{2,1,0:T(8,128)}, bf16[176,128,128]{2,1,0:T(8,128)(2,1)}, bf16[176,128,128]{2,1,0:T(8,128)(2,1)}) custom-call(s32[336]{0:T(512)S(1)} %squeeze.10.slots, s32[336]{0:T(512)S(1)} %squeeze.11.rows, s32[1]{0:T(128)} %get-tuple-element.44.steps, bf16[64,128,128]{2,1,0:T(8,128)(2,1)S(1)} %bitcast.24, ...), custom_call_target="tpu_custom_call" | custom-call | flops 2818572288 | bytes 69206016 | tf_op jit(solution)/shard_map/pull_back/pallas_call | solution.py:225
  365.7 0.6 collective-permute-start.4
  366.3 2.5 copy-done.2
  368.8 7.0 add_convert_fusion
  375.8 0.2 slice.80
  376.0 1.5 collective-permute-start.9
  377.5 62.9 %collective-permute-done.9 = bf16[88,128,128]{2,1,0:T(8,128)(2,1)S(1)} collective-permute-done((bf16[88,128,128]{2,1,0:T(8,128)(2,1)S(1)}, bf16[88,128,128]{2,1,0:T(8,128)(2,1)S(1)}, u32[]{:S(2)}, u32[]{:S(2)}) %collective-permute-start.9) | collective-permute-done | bytes 2883616 | tf_op jit(solution)/shard_map/ppermute | solution.py:143
  440.5 2.8 add_convert_fusion.2
  443.2 3.9 all-to-all-start.3
  447.1 7.0 add_convert_fusion.1
  454.1 0.2 slice.78
  454.3 1.5 collective-permute-start.5
  455.8 62.1 %collective-permute-done.5 = bf16[88,128,128]{2,1,0:T(8,128)(2,1)S(1)} collective-permute-done((bf16[88,128,128]{2,1,0:T(8,128)(2,1)S(1)}, bf16[88,128,128]{2,1,0:T(8,128)(2,1)S(1)}, u32[]{:S(2)}, u32[]{:S(2)}) %collective-permute-start.5) | collective-permute-done | bytes 2883616 | tf_op jit(solution)/shard_map/ppermute | solution.py:143
  517.9 2.7 add_convert_fusion.3
  520.7 5.6 all-to-all-start.2
  526.3 1.5 collective-permute-start.10
  527.9 61.8 %all-to-all-done.2 = bf16[8,11,128,128]{3,2,1,0:T(8,128)(2,1)} async-done(((bf16[8,11,128,128]{3,2,1,0:T(8,128)(2,1)}), bf16[8,11,128,128]{3,2,1,0:T(8,128)(2,1)}, u32[]{:S(2)}, u32[]{:S(2)}) %all-to-all-start.2) | async-done | bytes 2883616 | tf_op jit(solution)/shard_map/all_to_all | solution.py:150
  589.6 1.5 collective-permute-start.6
  591.1 4.8 pad_maximum_fusion.3.u_first
  595.9 55.2 %collective-permute-done.6 = bf16[88,128,128]{2,1,0:T(8,128)(2,1)S(1)} collective-permute-done((bf16[88,128,128]{2,1,0:T(8,128)(2,1)}, bf16[88,128,128]{2,1,0:T(8,128)(2,1)S(1)}, u32[]{:S(2)}, u32[]{:S(2)}) %collective-permute-start.6) | collective-permute-done | bytes 2883616 | tf_op jit(solution)/shard_map/ppermute | solution.py:143
  651.1 4.9 pad_maximum_fusion.2.g_first
  655.9 2.2 add_convert_fusion.4
  658.3 0.2 convert_reduce_fusion
  658.6 69.6 %reduce-scatter.2.cloned.1.call-done = bf16[8,128,128]{2,1,0:T(8,128)(2,1)} async-done(((bf16[64,128,128]{2,1,0:T(8,128)(2,1)}), bf16[8,128,128]{2,1,0:T(8,128)(2,1)}) %reduce-scatter.2.cloned.1.call-update) | async-done | bytes 262160 | tf_op jit(solution)/shard_map/reduce_scatter | solution.py:256
  728.2 1.1 copy.29
  729.4 0.9 copy.30
  730.2 19.4 %collect.1 = f32[2,168,128,128]{3,2,1,0:T(8,128)} custom-call(s32[336]{0:T(512)S(1)} %fusion.24.slots, bf16[176,128,128]{2,1,0:T(8,128)(2,1)} %pad_maximum_fusion.2.g_first, bf16[176,128,128]{2,1,0:T(8,128)(2,1)} %collective-permute-done.7.g_second, bf16[176,128,128]{2,1,0:T(8,128)(2,1)} %pad_maximum_fusion.3.u_first, ...), custom_call_target="tpu_custom_call" | custom-call | tf_op jit(solution)/shard_map/collect/pallas_call | solution.py:264
  (56 shorter events, 1.2 us)
Async XLA Ops:
  16.1 72.3 %all-to-all-start = ((bf16[8,11,128,128]{3,2,1,0:T(8,128)(2,1)}), bf16[8,11,128,128]{3,2,1,0:T(8,128)(2,1)S(1)}, u32[]{:S(2)}, u32[]{:S(2)}) async-start(bf16[8,11,128,128]{3,2,1,0:T(8,128)(2,1)} %bitcast.4), calls=%async_computation | async-start | bytes 5767168 | tf_op jit(solution)/shard_map/all_to_all | solution.py:150
  88.5 69.0 %all-to-all-start.1 = ((bf16[8,11,128,128]{3,2,1,0:T(8,128)(2,1)}), bf16[8,11,128,128]{3,2,1,0:T(8,128)(2,1)}, u32[]{:S(2)}, u32[]{:S(2)}) async-start(bf16[8,11,128,128]{3,2,1,0:T(8,128)(2,1)} %bitcast.6), calls=%async_computation.1 | async-start | bytes 5767168 | tf_op jit(solution)/shard_map/all_to_all | solution.py:150
  92.9 183.8 %all-gather.2.cloned.1.call-start = ((), (), s32[]{:S(2)}) async-start(), calls=%async_computation.5 | async-start | bytes 2359296 | tf_op jit(solution)/shard_map/all_gather | solution.py:174
  93.0 66.1 %collective-permute-start = (bf16[88,128,128]{2,1,0:T(8,128)(2,1)S(1)}, bf16[88,128,128]{2,1,0:T(8,128)(2,1)}, u32[]{:S(2)}, u32[]{:S(2)}) collective-permute-start(bf16[88,128,128]{2,1,0:T(8,128)(2,1)S(1)} %bitcast.27), channel_id=1, source_target_pairs={{0,16},{8,24},{16,0},{24,8},{1,17},{9,25},{17,1},{25,9},{2,18},{10... | collective-permute-start | bytes 8650760 | tf_op jit(solution)/shard_map/ppermute | solution.py:143
  157.5 62.8 %collective-permute-start.2 = (bf16[88,128,128]{2,1,0:T(8,128)(2,1)}, bf16[88,128,128]{2,1,0:T(8,128)(2,1)S(1)}, u32[]{:S(2)}, u32[]{:S(2)}) collective-permute-start(bf16[88,128,128]{2,1,0:T(8,128)(2,1)} %bitcast.7), channel_id=1, source_target_pairs={{0,16},{8,24},{16,0},{24,8},{1,17},{9,25},{17,1},{25,9},{2,18},{10... | collective-permute-start | bytes 8650760 | tf_op jit(solution)/shard_map/ppermute | solution.py:143
  163.8 61.3 %copy-start.6 = (bf16[128,1024]{1,0:T(8,128)(2,1)S(1)}, bf16[128,1024]{1,0:T(8,128)(2,1)}, u32[]{:S(2)}) copy-start(bf16[128,1024]{1,0:T(8,128)(2,1)} %param.5) | copy-start | bytes 786436
  163.8 117.1 %collective-permute-start.1 = (bf16[176,128,128]{2,1,0:T(8,128)(2,1)}, bf16[176,128,128]{2,1,0:T(8,128)(2,1)}, u32[]{:S(2)}, u32[]{:S(2)}) collective-permute-start(bf16[176,128,128]{2,1,0:T(8,128)(2,1)} %pad_maximum_fusion.first_ref), channel_id=1, source_target_pairs={{0,8},{8,0},{16,24},{24,16},{1,9},{9,1},{17,25},{25,17},{2,10},{10... | collective-permute-start | bytes 17301512 | tf_op jit(solution)/shard_map/ppermute | solution.py:137
  225.1 2.8 copy-start.7
  225.1 66.8 %collective-permute-start.3 = (bf16[176,128,128]{2,1,0:T(8,128)(2,1)}, bf16[176,128,128]{2,1,0:T(8,128)(2,1)}, u32[]{:S(2)}, u32[]{:S(2)}) collective-permute-start(bf16[176,128,128]{2,1,0:T(8,128)(2,1)} %pad_maximum_fusion.1.first_ref), channel_id=1, source_target_pairs={{0,8},{8,0},{16,24},{24,16},{1,9},{9,1},{17,25},{25,17},{2,10},{10... | collective-permute-start | bytes 17301512 | tf_op jit(solution)/shard_map/ppermute | solution.py:137
  276.7 4.2 copy-start
  291.9 21.0 %copy-start.5 = (bf16[128,3584]{1,0:T(8,128)(2,1)S(1)}, bf16[128,3584]{1,0:T(8,128)(2,1)}, u32[]{:S(2)}) copy-start(bf16[128,3584]{1,0:T(8,128)(2,1)} %param.6) | copy-start | bytes 2752516
  312.9 2.0 copy-start.1
  346.6 19.7 %collective-permute-start.8 = (bf16[176,128,128]{2,1,0:T(8,128)(2,1)}, bf16[176,128,128]{2,1,0:T(8,128)(2,1)S(1)}, u32[]{:S(2)}, u32[]{:S(2)}) collective-permute-start(bf16[176,128,128]{2,1,0:T(8,128)(2,1)} %get-tuple-element.14), channel_id=1, source_target_pairs={{0,8},{8,0},{16,24},{24,16},{1,9},{9,1},{17,25},{25,17},{2,10},{10... | collective-permute-start | bytes 17301512 | tf_op jit(solution)/shard_map/ppermute | solution.py:137
  365.7 81.4 %collective-permute-start.4 = (bf16[176,128,128]{2,1,0:T(8,128)(2,1)}, bf16[176,128,128]{2,1,0:T(8,128)(2,1)}, u32[]{:S(2)}, u32[]{:S(2)}) collective-permute-start(bf16[176,128,128]{2,1,0:T(8,128)(2,1)} %get-tuple-element.12), channel_id=1, source_target_pairs={{0,8},{8,0},{16,24},{24,16},{1,9},{9,1},{17,25},{25,17},{2,10},{10... | collective-permute-start | bytes 17301512 | tf_op jit(solution)/shard_map/ppermute | solution.py:137
  366.3 2.5 copy-start.2
  376.0 64.5 %collective-permute-start.9 = (bf16[88,128,128]{2,1,0:T(8,128)(2,1)S(1)}, bf16[88,128,128]{2,1,0:T(8,128)(2,1)S(1)}, u32[]{:S(2)}, u32[]{:S(2)}) collective-permute-start(bf16[88,128,128]{2,1,0:T(8,128)(2,1)S(1)} %slice.80), channel_id=1, source_target_pairs={{0,16},{8,24},{16,0},{24,8},{1,17},{9,25},{17,1},{25,9},{2,18},{10... | collective-permute-start | bytes 8650760 | tf_op jit(solution)/shard_map/ppermute | solution.py:143
  443.2 77.4 %all-to-all-start.3 = ((bf16[8,11,128,128]{3,2,1,0:T(8,128)(2,1)}), bf16[8,11,128,128]{3,2,1,0:T(8,128)(2,1)S(1)}, u32[]{:S(2)}, u32[]{:S(2)}) async-start(bf16[8,11,128,128]{3,2,1,0:T(8,128)(2,1)} %bitcast.13), calls=%async_computation.4 | async-start | bytes 5767168 | tf_op jit(solution)/shard_map/all_to_all | solution.py:150
  454.3 63.6 %collective-permute-start.5 = (bf16[88,128,128]{2,1,0:T(8,128)(2,1)S(1)}, bf16[88,128,128]{2,1,0:T(8,128)(2,1)S(1)}, u32[]{:S(2)}, u32[]{:S(2)}) collective-permute-start(bf16[88,128,128]{2,1,0:T(8,128)(2,1)S(1)} %slice.78), channel_id=1, source_target_pairs={{0,16},{8,24},{16,0},{24,8},{1,17},{9,25},{17,1},{25,9},{2,18},{10... | collective-permute-start | bytes 8650760 | tf_op jit(solution)/shard_map/ppermute | solution.py:143
  520.7 69.0 %all-to-all-start.2 = ((bf16[8,11,128,128]{3,2,1,0:T(8,128)(2,1)}), bf16[8,11,128,128]{3,2,1,0:T(8,128)(2,1)}, u32[]{:S(2)}, u32[]{:S(2)}) async-start(bf16[8,11,128,128]{3,2,1,0:T(8,128)(2,1)} %bitcast.11), calls=%async_computation.3 | async-start | bytes 5767168 | tf_op jit(solution)/shard_map/all_to_all | solution.py:150
  526.3 201.9 %reduce-scatter.2.cloned.1.call-start = ((), (), s32[]{:S(2)}) async-start(), calls=%async_computation.6 | async-start | bytes 2359296 | tf_op jit(solution)/shard_map/reduce_scatter | solution.py:256
  526.3 64.8 %collective-permute-start.10 = (bf16[88,128,128]{2,1,0:T(8,128)(2,1)S(1)}, bf16[88,128,128]{2,1,0:T(8,128)(2,1)}, u32[]{:S(2)}, u32[]{:S(2)}) collective-permute-start(bf16[88,128,128]{2,1,0:T(8,128)(2,1)S(1)} %bitcast.25), channel_id=1, source_target_pairs={{0,16},{8,24},{16,0},{24,8},{1,17},{9,25},{17,1},{25,9},{2,18},{10... | collective-permute-start | bytes 8650760 | tf_op jit(solution)/shard_map/ppermute | solution.py:143
  589.6 61.4 %collective-permute-start.6 = (bf16[88,128,128]{2,1,0:T(8,128)(2,1)}, bf16[88,128,128]{2,1,0:T(8,128)(2,1)S(1)}, u32[]{:S(2)}, u32[]{:S(2)}) collective-permute-start(bf16[88,128,128]{2,1,0:T(8,128)(2,1)} %bitcast.12), channel_id=1, source_target_pairs={{0,16},{8,24},{16,0},{24,8},{1,17},{9,25},{17,1},{25,9},{2,18},{10... | collective-permute-start | bytes 8650760 | tf_op jit(solution)/shard_map/ppermute | solution.py:143
  595.9 60.0 %copy-start.3 = (f32[64,128,128]{2,1,0:T(8,128)S(1)}, f32[64,128,128]{2,1,0:T(8,128)}, u32[]{:S(2)}) copy-start(f32[64,128,128]{2,1,0:T(8,128)} %get-tuple-element.10) | copy-start | bytes 12582916
  595.9 60.0 %copy-start.4 = (f32[64,128,128]{2,1,0:T(8,128)S(1)}, f32[64,128,128]{2,1,0:T(8,128)}, u32[]{:S(2)}) copy-start(f32[64,128,128]{2,1,0:T(8,128)} %get-tuple-element.9) | copy-start | bytes 12582916
  595.9 134.3 %collective-permute-start.11 = (bf16[176,128,128]{2,1,0:T(8,128)(2,1)}, bf16[176,128,128]{2,1,0:T(8,128)(2,1)}, u32[]{:S(2)}, u32[]{:S(2)}) collective-permute-start(bf16[176,128,128]{2,1,0:T(8,128)(2,1)} %pad_maximum_fusion.3.u_first), channel_id=1, source_target_pairs={{0,8},{8,0},{16,24},{24,16},{1,9},{9,1},{17,25},{25,17},{2,10},{10... | collective-permute-start | bytes 17301512 | tf_op jit(solution)/shard_map/ppermute | solution.py:137
  655.9 74.3 %collective-permute-start.7 = (bf16[176,128,128]{2,1,0:T(8,128)(2,1)}, bf16[176,128,128]{2,1,0:T(8,128)(2,1)}, u32[]{:S(2)}, u32[]{:S(2)}) collective-permute-start(bf16[176,128,128]{2,1,0:T(8,128)(2,1)} %pad_maximum_fusion.2.g_first), channel_id=1, source_target_pairs={{0,8},{8,0},{16,24},{24,16},{1,9},{9,1},{17,25},{25,17},{2,10},{10... | collective-permute-start | bytes 17301512 | tf_op jit(solution)/shard_map/ppermute | solution.py:137
Sparse Core Ops, SparseCore 0:
  226.3 50.3 all-gather.1
  658.3 69.8 reduce-scatter.1

commit v2 on v1

v2 whole, which is shorter than its diff:
```python
import functools

import jax
import jax.numpy as jnp
from jax import lax
from jax.experimental import pallas as pl
from jax.experimental.pallas import tpu as pltpu
from jax.sharding import PartitionSpec as P

KHEAVY = 12
KLIGHT = 4
CORES = 2
VMEM_BYTES = 50 * 1024 * 1024


def load_pieces(pieces, buf, sems):
    offset = 0
    copies = []
    for i, piece in enumerate(pieces):
        count = piece.shape[0]
        copies.append(pltpu.make_async_copy(piece, buf.at[pl.ds(offset, count)], sems.at[i]))
        offset += count
    for copy in copies:
        copy.start()
    for copy in copies:
        copy.wait()


def forward_kernel(slots, rows, steps, tok_ref, *refs):
    pieces, (pre_ref, buf, sems) = refs[:-3], refs[-3:]
    load_pieces(pieces, buf, sems)
    size = tok_ref.shape[-1]
    panels = pre_ref.shape[1] // size

    def panel_step(p, carry):
        def group(t, total):
            base = p * KHEAVY + t * KLIGHT
            left = jnp.concatenate([tok_ref[rows[base + i]] for i in range(KLIGHT)], axis=1)
            right = jnp.concatenate([buf[slots[base + i]] for i in range(KLIGHT)], axis=0)
            return total + jnp.dot(left, right, preferred_element_type=jnp.float32)

        total = lax.fori_loop(0, steps[0], group, jnp.zeros((tok_ref.shape[1], size), jnp.float32))
        pre_ref[:, pl.ds(pl.multiple_of(p * size, size), size)] = total
        return carry

    lax.fori_loop(0, panels, panel_step, 0)


def backward_kernel(first, count, slots, rows, steps, tokt_ref, grad_ref, *refs):
    prior = () if first else refs[:1]
    refs = refs[len(prior) :]
    pieces, terms_out, outs = refs[:count], refs[count], refs[count + 1 : 2 * count + 1]
    buf, grads, sems = refs[2 * count + 1 : 2 * count + 4]
    terms_ref = terms_out if first else refs[-1]
    load_pieces(pieces, buf, sems)
    size = tokt_ref.shape[1]
    panels = grad_ref.shape[1] // size
    terms_ref[...] = jnp.zeros_like(terms_ref) if first else prior[0][...]

    def panel_step(p, carry):
        column = grad_ref[:, pl.ds(pl.multiple_of(p * size, size), size)]

        def group(t, inner):
            base = p * KHEAVY + t * KLIGHT
            row = [rows[base + i] for i in range(KLIGHT)]
            slot = [slots[base + i] for i in range(KLIGHT)]
            weight = jnp.concatenate([buf[s] for s in slot], axis=0)
            back = lax.dot_general(
                column, weight, (((1,), (1,)), ((), ())), preferred_element_type=jnp.float32
            )
            picked = jnp.concatenate([tokt_ref[r] for r in row], axis=0)
            outer = jnp.dot(picked, column, preferred_element_type=jnp.float32).astype(grads.dtype)
            before = [terms_ref[r] for r in row]
            for i in range(KLIGHT):
                terms_ref[row[i]] = before[i] + back[:, i * size : (i + 1) * size]
                grads[slot[i]] = outer[i * size : (i + 1) * size]
            return inner

        return lax.fori_loop(0, steps[0], group, carry)

    lax.fori_loop(0, panels, panel_step, 0)
    offset = 0
    copies = []
    for i, out in enumerate(outs):
        copies.append(
            pltpu.make_async_copy(grads.at[pl.ds(offset, out.shape[0])], out, sems.at[i])
        )
        offset += out.shape[0]
    for copy in copies:
        copy.start()
    if not first:
        terms_out[...] = terms_ref[...].astype(terms_out.dtype)
    for copy in copies:
        copy.wait()


def collect_kernel(slots, *refs):
    pieces, (out_ref, buf, sems) = refs[:-3], refs[-3:]
    m, c = pl.program_id(0), pl.program_id(1)
    each = len(pieces) // 2

    @pl.when((m == 0) & (c == 0))
    def _():
        load_pieces(pieces[:each], buf, sems)

    @pl.when((m == 1) & (c == 0))
    def _():
        load_pieces(pieces[each:], buf, sems)

    chunk = out_ref.shape[1]
    owned = chunk * pl.num_programs(1)

    def step(i, carry):
        out_ref[0, i] = buf[slots[m * owned + c * chunk + i]].astype(jnp.float32)
        return carry

    lax.fori_loop(0, chunk, step, 0, unroll=True)


def per_device(tokens, cotangent, tiles, tile_rows, tile_cols):
    members = lax.axis_size("mp")
    myself = lax.axis_index("mp")
    groups = lax.axis_size("dp")
    group_id = lax.axis_index("dp")
    lanes = groups // CORES
    my_y, my_core = group_id // CORES, group_id % CORES
    size = tiles.shape[-1]
    owned = tiles.shape[1]
    tok_rows = tokens.shape[0]
    local_blocks = tokens.shape[1] // size
    row_blocks = local_blocks * members
    panels = cotangent.shape[1] // size
    capacity = (panels * KHEAVY + members - 1) // members
    share = (capacity + groups - 1) // groups
    parts = [(0, (share + 1) // 2), ((share + 1) // 2, share // 2)]
    parts = [(low, count) for low, count in parts if count]
    packed = (owned + groups - 1) // groups
    slot_count = groups * members * share
    smem = pl.BlockSpec(memory_space=pltpu.SMEM)
    vmem = pl.BlockSpec(memory_space=pltpu.VMEM)
    anywhere = pl.BlockSpec(memory_space=pl.ANY)
    ints = jnp.int32

    def piece_of(tile):
        sender = tile % groups
        core_off = (sender % CORES + my_core) % CORES
        y_off = (my_y - sender // CORES + lanes) % lanes
        return core_off * lanes + y_off

    def skipped(start, sender):
        return (start - sender + groups - 1) // groups

    def place(piece, partner, q):
        found, base = 0, 0
        for low, count in parts:
            here = base + (piece * members + partner) * count + q - low
            found = jnp.where(q >= low, here, found)
            base += groups * members * count
        return found

    def swap_cores(x):
        pairs = [(d, d - 1 if d % CORES else d + 1) for d in range(groups)]
        return lax.ppermute(x, "dp", pairs)

    def shift_y(x, by):
        pairs = [
            (d, ((d // CORES + by) % lanes) * CORES + d % CORES) for d in range(groups)
        ]
        return lax.ppermute(x, "dp", pairs)

    def spread(x):
        mine = [x] + [shift_y(x, s) for s in range(1, lanes)]
        return mine + [swap_cores(piece) for piece in mine]

    def exchange(x):
        swapped = lax.all_to_all(
            x.reshape(members, -1, size, size), "mp", split_axis=0, concat_axis=0, tiled=True
        )
        return swapped.reshape(-1, size, size)

    cols_all = tile_cols.reshape(2, members, owned)
    holder_all = cols_all // panels
    my_holder = lax.dynamic_index_in_dim(holder_all, myself, 1, keepdims=False)
    member_ids = jnp.arange(members, dtype=ints)
    tile_ids = jnp.arange(owned, dtype=ints)
    start = jnp.sum((my_holder[:, None, :] < member_ids[None, :, None]).astype(ints), axis=2)
    lead = skipped(start, group_id)
    flat_tiles = tiles.reshape(2 * owned, size, size)
    landed = []
    for m in range(2):
        for low, count in parts:
            source = (lead[m][:, None] + low + jnp.arange(count, dtype=ints)[None, :]) * groups
            source = jnp.minimum(source + group_id, owned - 1) + m * owned
            picked = jnp.take(flat_tiles, source.reshape(-1), axis=0, mode="clip")
            landed.append(exchange(picked))

    blocks = jnp.transpose(tokens.reshape(tok_rows, local_blocks, size), (1, 0, 2))
    tok = lax.all_gather(blocks, "mp", axis=0, tiled=True)
    tokt = jnp.transpose(tok, (0, 2, 1))

    first = jnp.sum((holder_all < myself).astype(ints), axis=2)[:, :, None]
    owner_tile = tile_ids[None, None, :]
    q_all = owner_tile // groups - skipped(first, owner_tile % groups)
    slot_all = place(piece_of(owner_tile), member_ids[None, :, None], q_all).reshape(2, -1)
    local_cols = tile_cols - myself * panels
    mask = local_cols[:, None, :] == jnp.arange(panels, dtype=ints)[None, :, None]
    listed = jnp.arange(tile_cols.shape[1])
    before = (listed[:, None] < listed[None, :]).astype(jnp.bfloat16)
    rank = jnp.einsum(
        "mpk,kl->mpl", mask.astype(jnp.bfloat16), before, preferred_element_type=jnp.float32
    ).astype(ints)
    chosen = mask[:, :, None, :] & (
        rank[:, :, None, :] == jnp.arange(KHEAVY, dtype=ints)[None, None, :, None]
    )
    slots = jnp.sum(jnp.where(chosen, slot_all[:, None, None, :], 0), axis=3).reshape(2, -1)
    rows = jnp.sum(jnp.where(chosen, tile_rows[:, None, None, :], 0), axis=3).reshape(2, -1)
    steps = jnp.sum(mask[:, 0, :].astype(ints), axis=1) // KLIGHT

    landed[-1], tok, tokt, slots, rows, steps = lax.optimization_barrier(
        (landed[-1], tok, tokt, slots, rows, steps)
    )
    per_matrix = len(parts)
    arrived = [
        sum([spread(x) for x in landed[m * per_matrix : (m + 1) * per_matrix]], [])
        for m in range(2)
    ]
    piece_count = per_matrix * groups

    slot_bytes = slot_count * size * size * 2
    flops = 2 * panels * KHEAVY * size**2 * tok_rows
    tile_buf = pltpu.VMEM((slot_count, size, size), jnp.bfloat16)
    piece_sems = pltpu.SemaphoreType.DMA((piece_count,))
    params = pltpu.CompilerParams(vmem_limit_bytes=VMEM_BYTES)

    def project(m):
        return pl.pallas_call(
            forward_kernel,
            out_shape=jax.ShapeDtypeStruct(cotangent.shape, jnp.float32),
            in_specs=[smem, smem, smem, vmem] + [anywhere] * piece_count,
            out_specs=vmem,
            scratch_shapes=[tile_buf, piece_sems],
            compiler_params=params,
            cost_estimate=pl.CostEstimate(
                flops=flops, bytes_accessed=4 * slot_bytes, transcendentals=0
            ),
            name="project",
        )(slots[m], rows[m], steps[m : m + 1], tok, *arrived[m])

    gate_pre, up_pre = project(0), project(1)
    sigmoid_gate = jax.nn.sigmoid(gate_pre)
    hidden = (gate_pre * sigmoid_gate * up_pre).astype(jnp.bfloat16)
    upstream = cotangent.astype(jnp.float32)
    gate_grad = (upstream * up_pre * sigmoid_gate * (1.0 + gate_pre * (1.0 - sigmoid_gate))).astype(
        jnp.bfloat16
    )
    up_grad = (upstream * gate_pre * sigmoid_gate).astype(jnp.bfloat16)

    terms_shape = (row_blocks, tok_rows, size)

    def pull_back(m, grad, prior):
        begin = not prior
        piece_shapes = [jax.ShapeDtypeStruct(x.shape, jnp.bfloat16) for x in arrived[m]]
        terms_type = jnp.float32 if begin else jnp.bfloat16
        scratch = [tile_buf, tile_buf, piece_sems]
        results = pl.pallas_call(
            functools.partial(backward_kernel, begin, piece_count),
            out_shape=[jax.ShapeDtypeStruct(terms_shape, terms_type)] + piece_shapes,
            in_specs=[smem, smem, smem] + [vmem] * (2 + len(prior)) + [anywhere] * piece_count,
            out_specs=[vmem] + [anywhere] * piece_count,
            scratch_shapes=scratch if begin else scratch + [pltpu.VMEM(terms_shape, jnp.float32)],
            compiler_params=params,
            cost_estimate=pl.CostEstimate(
                flops=2 * flops, bytes_accessed=6 * slot_bytes, transcendentals=0
            ),
            name="pull_back",
        )(slots[m], rows[m], steps[m : m + 1], tokt, grad, *prior, *arrived[m])
        return results[0], results[1:]

    def add_pair(x, y):
        return x.astype(jnp.float32) + y.astype(jnp.float32)

    def total_of(pieces):
        pair = [
            add_pair(pieces[s], swap_cores(pieces[lanes + s])).astype(jnp.bfloat16)
            for s in range(lanes)
        ]
        total = pair[0].astype(jnp.float32)
        for s in range(1, lanes):
            total = total + shift_y(pair[s], lanes - s).astype(jnp.float32)
        return exchange(total.astype(jnp.bfloat16))

    def totals_of(pieces):
        return [total_of(pieces[i * groups : (i + 1) * groups]) for i in range(per_matrix)]

    def pack(m, returned):
        held = jnp.minimum(jnp.arange(packed, dtype=ints) * groups + group_id, owned - 1)
        holder = jnp.take(my_holder[m], held, mode="clip")
        q = held // groups - jnp.take(lead[m], holder, mode="clip")
        found, base = 0, 0
        for low, count in parts:
            found = jnp.where(q >= low, base + holder * count + q - low, found)
            base += members * count
        return jnp.take(jnp.concatenate(returned, axis=0), found, axis=0, mode="clip")

    gate_terms, gate_pieces = pull_back(0, gate_grad, [])
    terms, up_pieces = pull_back(1, up_grad, [gate_terms])
    gate_back = pack(0, totals_of(gate_pieces))
    up_back = pack(1, totals_of(up_pieces))
    mine = lax.psum_scatter(terms, "mp", scatter_dimension=0, tiled=True)
    up_back, mine = lax.optimization_barrier((up_back, mine))
    home_pieces = spread(gate_back) + spread(up_back)
    input_grad = jnp.transpose(mine, (1, 0, 2)).reshape(tokens.shape)

    home = piece_of(tile_ids) * packed + tile_ids // groups
    chunk = max(c for c in range(1, 29) if owned % c == 0)
    tile_grads = pl.pallas_call(
        collect_kernel,
        out_shape=jax.ShapeDtypeStruct(tiles.shape, jnp.float32),
        grid=(2, owned // chunk),
        in_specs=[smem] + [anywhere] * (2 * groups),
        out_specs=pl.BlockSpec((1, chunk, size, size), lambda m, c: (m, c, 0, 0)),
        scratch_shapes=[
            pltpu.VMEM((groups * packed, size, size), jnp.bfloat16),
            pltpu.SemaphoreType.DMA((groups,)),
        ],
        compiler_params=params,
        name="collect",
    )(jnp.concatenate([home, home]), *home_pieces)
    return (hidden, input_grad, tile_grads)


def solution(mesh):
    in_specs = (P("dp", "mp"), P("dp", "mp"), P(None, "mp", None, None), P(), P())
    out_specs = (P("dp", "mp"), P("dp", "mp"), P(None, "mp", None, None))
    return jax.shard_map(
        per_device, mesh=mesh, in_specs=in_specs, out_specs=out_specs, check_vma=False
    )
```

time: 757 us -> 649 us (0.86)
  waiting for transfers between devices: 523 us -> 374 us
  starting transfers between devices: 31.1 us -> 64.3 us
  local copies, waits for them, and re-layouts: 28.2 us -> 46.7 us
    reduce_scatter x1, waiting for transfers between devices: 69.6 us -> 0.01 us  [per_device(): mine = lax.psum_scatter(terms, 'mp', scatter_dimension=0, tiled=True)]
    all_to_all x4 -> x8, waiting for transfers between devices: 183 us -> 127 us  [exchange(): lax.all_to_all(x.reshape(members, -1, size, size), 'mp', split_axis=0, co...]
    all_to_all x4 -> x8, starting transfers between devices: 21.2 us -> 52.1 us  [exchange(): lax.all_to_all(x.reshape(members, -1, size, size), 'mp', split_axis=0, co...]
    all_gather x1, waiting for transfers between devices: 33.6 us -> 7.92 us  [per_device(): tok = lax.all_gather(blocks, 'mp', axis=0, tiled=True)]
    gather x2 -> x9, local copies, waits for them, and re-layouts: 13.5 us -> 32.8 us  [the longest x4 24.2 us: per_device(): picked = jnp.take(flat_tiles, source.reshape(-1), axis=0, mode='clip')]
    concatenate x4 -> x3, other arithmetic: 19.3 us -> 6.85 us  [the longest x2 6.78 us: pack(): jnp.concatenate(returned, axis=0)]
    select_n x1 -> x6, other arithmetic: 0.01 us -> 10 us  [the longest x2 9.96 us: pack(): found = jnp.where(q >= low, base + holder * count + q - low, found)]
    convert_element_type x5 -> x8, other arithmetic: 21.6 us -> 18.1 us  [the longest x4 10.7 us: total_of(): return exchange(total.astype(jnp.bfloat16))]
  transfers between devices with their start and end apart: 18 -> 40, of which waited for: 9 -> 20; matrix products, arithmetic and copies ran while one was open for 10% -> 13% of each run, Pallas kernels for 4% -> 7%
where the time goes in v2:
time: 649 us; the launch traced here: 654 us
  waiting for transfers between devices  374 us (58%)
  Pallas kernels  101 us (16%)
  starting transfers between devices  64.3 us (10%)
  other arithmetic  52.6 us (8%)
  local copies, waits for them, and re-layouts  46.7 us (7%)
  between operations  14.6 us (2%)
    ppermute x10, waiting for transfers between devices, shift_y(): return lax.ppermute(x, 'dp', pairs)  234 us
    all_to_all x8, waiting for transfers between devices, exchange(): lax.all_to_all(x.reshape(members, -1, size, size), 'mp', split_axis=0, co...  127 us
    all_to_all x8, starting transfers between devices, exchange(): lax.all_to_all(x.reshape(members, -1, size, size), 'mp', split_axis=0, co...  52.1 us
    pallas_call x2, Pallas kernels, pull_back(): pl.pallas_call(functools.partial(backward_kernel, begin, piece_count), ou...  51.9 us
    pallas_call x2, Pallas kernels, project(): pl.pallas_call(forward_kernel, out_shape=jax.ShapeDtypeStruct(cotangent.s...  35.2 us
    gather x4, local copies, waits for them, and re-layouts, per_device(): picked = jnp.take(flat_tiles, source.reshape(-1), axis=0, mode='clip')  24.2 us
    pallas_call x1, Pallas kernels, per_device(): pl.pallas_call(collect_kernel, out_shape=jax.ShapeDtypeStruct(tiles.shape...  14.1 us
  transfers between devices with their start and end apart: 40, of which 20 were waited for; matrix products, arithmetic and copies ran while one was open for 13% of the time, Pallas kernels for 7%

profile of v2, /device:TPU:0, one launch (start us, length us, event | category | flops | bytes accessed | tf_op | source)
XLA Modules:
  0.0 653.8 jit_solution(11924188613182822216)
XLA Ops:
  7.2 0.7 compare_and_fusion.1
  7.9 0.7 broadcast_subtract_fusion
  9.4 6.0 gather_fusion.2
  15.3 7.3 %all-to-all-start.2 = ((bf16[8,5,128,128]{3,2,1,0:T(8,128)(2,1)}), bf16[8,5,128,128]{3,2,1,0:T(8,128)(2,1)S(1)}, u32[]{:S(2)}, u32[]{:S(2)}) async-start(bf16[8,5,128,128]{3,2,1,0:T(8,128)(2,1)} %bitcast.11), calls=%async_computation.2 | async-start | bytes 2621440 | tf_op jit(solution)/shard_map/all_to_all | solution.py:176
  22.8 6.1 gather_fusion.1
  28.9 25.1 %all-to-all-done.2 = bf16[8,5,128,128]{3,2,1,0:T(8,128)(2,1)S(1)} async-done(((bf16[8,5,128,128]{3,2,1,0:T(8,128)(2,1)}), bf16[8,5,128,128]{3,2,1,0:T(8,128)(2,1)S(1)}, u32[]{:S(2)}, u32[]{:S(2)}) %all-to-all-start.2) | async-done | bytes 1310752 | tf_op jit(solution)/shard_map/all_to_all | solution.py:176
  54.0 4.3 all-to-all-start.1
  58.4 6.1 gather_fusion.3
  64.5 30.5 %all-to-all-done.1 = bf16[8,6,128,128]{3,2,1,0:T(8,128)(2,1)} async-done(((bf16[8,6,128,128]{3,2,1,0:T(8,128)(2,1)}), bf16[8,6,128,128]{3,2,1,0:T(8,128)(2,1)}, u32[]{:S(2)}, u32[]{:S(2)}) %all-to-all-start.1) | async-done | bytes 1572896 | tf_op jit(solution)/shard_map/all_to_all | solution.py:176
  94.9 4.4 all-to-all-start.3
  99.6 0.9 copy.25
  101.2 6.0 gather_fusion
  107.2 37.2 %all-to-all-done.3 = bf16[8,6,128,128]{3,2,1,0:T(8,128)(2,1)} async-done(((bf16[8,6,128,128]{3,2,1,0:T(8,128)(2,1)}), bf16[8,6,128,128]{3,2,1,0:T(8,128)(2,1)}, u32[]{:S(2)}, u32[]{:S(2)}) %all-to-all-start.3) | async-done | bytes 1572896 | tf_op jit(solution)/shard_map/all_to_all | solution.py:176
  144.4 3.8 all-to-all-start
  148.3 1.6 collective-permute-start.3
  151.7 1.5 collective-permute-start.6
  153.2 11.9 %select_reduce_fusion = (s32[2,28,12]{0,2,1:T(8,128)S(1)}, s32[2,28,12]{0,2,1:T(8,128)S(1)}) fusion(pred[2,28,1344]{2,0,1:T(4,128)(4,1)S(1)} %copy.27, s32[2,1344]{1,0:T(2,128)S(1)} %copy-done.15, s32[2,28,1344]{2,0,1:T(2,128)S(1)} %copy.28, s32[2,1344]{1,0:T(2,128)S(1)} %compare_select_fusion.1), kind=kLoop, calls=%fused_computation.12 | loop fusion | flops 5417664 | bytes 403200 | tf_op jit(solution)/shard_map/reduce_sum | solution.py:216
  166.1 14.1 %collective-permute-done.3.refs_5_ = bf16[40,128,128]{2,1,0:T(8,128)(2,1)} collective-permute-done((bf16[40,128,128]{2,1,0:T(8,128)(2,1)S(1)}, bf16[40,128,128]{2,1,0:T(8,128)(2,1)}, u32[]{:S(2)}, u32[]{:S(2)}) %collective-permute-start.3) | collective-permute-done | bytes 1310752 | tf_op jit(solution)/shard_map/ppermute | solution.py:169
  180.2 7.9 %all-gather.2.cloned.1.call-done.tok_ref = bf16[64,128,128]{2,1,0:T(8,128)(2,1)} async-done(((bf16[8,128,128]{2,1,0:T(8,128)(2,1)}), bf16[64,128,128]{2,1,0:T(8,128)(2,1)}) %all-gather.2.cloned.1.call-update) | async-done | bytes 2097168 | tf_op jit(solution)/shard_map/all_gather | solution.py:198
  188.1 4.1 copy.26
  192.7 1.5 collective-permute-start.9
  194.2 19.7 %collective-permute-done.refs_1_ = bf16[48,128,128]{2,1,0:T(8,128)(2,1)} collective-permute-done((bf16[48,128,128]{2,1,0:T(8,128)(2,1)}, bf16[48,128,128]{2,1,0:T(8,128)(2,1)}, u32[]{:S(2)}, u32[]{:S(2)}) %collective-permute-start) | collective-permute-done | bytes 1572896 | tf_op jit(solution)/shard_map/ppermute | solution.py:169
  214.4 33.2 %collective-permute-done.6.refs_1_.refs_2_ = bf16[48,128,128]{2,1,0:T(8,128)(2,1)} collective-permute-done((bf16[48,128,128]{2,1,0:T(8,128)(2,1)}, bf16[48,128,128]{2,1,0:T(8,128)(2,1)}, u32[]{:S(2)}, u32[]{:S(2)}) %collective-permute-start.6) | collective-permute-done | bytes 1572896 | tf_op jit(solution)/shard_map/ppermute | solution.py:169
  248.1 26.0 %collective-permute-done.9.refs_5_.refs_6_ = bf16[40,128,128]{2,1,0:T(8,128)(2,1)S(1)} collective-permute-done((bf16[40,128,128]{2,1,0:T(8,128)(2,1)S(1)}, bf16[40,128,128]{2,1,0:T(8,128)(2,1)S(1)}, u32[]{:S(2)}, u32[]{:S(2)}) %collective-permute-start.9) | collective-permute-done | bytes 1310752 | tf_op jit(solution)/shard_map/ppermute | solution.py:169
  274.9 1.2 copy-done.7
  276.0 22.9 %project.2 = f32[128,3584]{1,0:T(8,128)} custom-call(s32[336]{0:T(512)S(1)} %get-tuple-element.71.slots, s32[336]{0:T(512)S(1)} %get-tuple-element.69.rows, s32[1]{0:T(128)} %get-tuple-element.104.steps, bf16[64,128,128]{2,1,0:T(8,128)(2,1)} %all-gather.2.cloned.1.call-done.tok_ref, bf16[48,128,128]{2,1,0:T(8,128)(2,1)} %bitcast.10.refs_0_, ...), custom_call_target="tpu_custom_call" | custom-call | flops 1409286144 | bytes 46137344 | tf_op jit(solution)/shard_map/project/pallas_call | solution.py:236
  299.1 1.6 copy-done.5
  300.6 12.3 %project.3 = f32[128,3584]{1,0:T(8,128)} custom-call(s32[336]{0:T(512)S(1)} %get-tuple-element.72.slots, s32[336]{0:T(512)S(1)} %get-tuple-element.70.rows, s32[1]{0:T(128)} %get-tuple-element.105.steps, bf16[64,128,128]{2,1,0:T(8,128)(2,1)} %all-gather.2.cloned.1.call-done.tok_ref, bf16[48,128,128]{2,1,0:T(8,128)(2,1)} %bitcast.14.refs_0_.refs_1_, ...), custom_call_target="tpu_custom_call" | custom-call | flops 1409286144 | bytes 46137344 | tf_op jit(solution)/shard_map/project/pallas_call | solution.py:236
  313.0 3.5 fusion.10
  316.5 32.3 %pull_back.2 = (f32[64,128,128]{2,1,0:T(8,128)}, bf16[48,128,128]{2,1,0:T(8,128)(2,1)}, bf16[48,128,128]{2,1,0:T(8,128)(2,1)}, bf16[48,128,128]{2,1,0:T(8,128)(2...) custom-call(s32[336]{0:T(512)S(1)} %get-tuple-element.71.slots, ...), custom_call_target="tpu_custom_call" | custom-call | flops 2818572288 | bytes 69206016 | tf_op jit(solution)/shard_map/pull_back/pallas_call | solution.py:265
  349.4 2.8 collective-permute-done.22
  352.6 1.6 collective-permute-start.23
  354.2 19.6 %pull_back.3 = (bf16[64,128,128]{2,1,0:T(8,128)(2,1)}, bf16[48,128,128]{2,1,0:T(8,128)(2,1)}, bf16[48,128,128]{2,1,0:T(8,128)(2,1)}, bf16[48,128,128]{2,1,0:T(8,...) custom-call(s32[336]{0:T(512)S(1)} %get-tuple-element.72.slots, ...), custom_call_target="tpu_custom_call" | custom-call | flops 2818572288 | bytes 69206016 | tf_op jit(solution)/shard_map/pull_back/pallas_call | solution.py:265
  374.0 9.7 %collective-permute-done.23 = bf16[40,128,128]{2,1,0:T(8,128)(2,1)S(1)} collective-permute-done((bf16[40,128,128]{2,1,0:T(8,128)(2,1)S(1)}, bf16[40,128,128]{2,1,0:T(8,128)(2,1)S(1)}, u32[]{:S(2)}, u32[]{:S(2)}) %collective-permute-start.23) | collective-permute-done | bytes 1310752 | tf_op jit(solution)/shard_map/ppermute | solution.py:169
  383.8 1.7 add_convert_fusion.6
  385.4 16.2 %all-to-all-start.7 = ((bf16[8,5,128,128]{3,2,1,0:T(8,128)(2,1)}), bf16[8,5,128,128]{3,2,1,0:T(8,128)(2,1)}, u32[]{:S(2)}, u32[]{:S(2)}) async-start(bf16[8,5,128,128]{3,2,1,0:T(8,128)(2,1)} %bitcast.108), calls=%async_computation.8 | async-start | bytes 2621440 | tf_op jit(solution)/shard_map/all_to_all | solution.py:176
  401.8 1.8 add_convert_fusion.10
  404.9 29.8 %collective-permute-done.17 = bf16[40,128,128]{2,1,0:T(8,128)(2,1)S(1)} collective-permute-done((bf16[40,128,128]{2,1,0:T(8,128)(2,1)S(1)}, bf16[40,128,128]{2,1,0:T(8,128)(2,1)S(1)}, u32[]{:S(2)}, u32[]{:S(2)}) %collective-permute-start.17) | collective-permute-done | bytes 1310752 | tf_op jit(solution)/shard_map/ppermute | solution.py:169
  434.7 1.7 add_convert_fusion.9
  436.4 6.1 all-to-all-start.5
  442.6 2.1 add_convert_fusion.1
  445.2 35.2 %collective-permute-done.20 = bf16[48,128,128]{2,1,0:T(8,128)(2,1)S(1)} collective-permute-done((bf16[48,128,128]{2,1,0:T(8,128)(2,1)S(1)}, bf16[48,128,128]{2,1,0:T(8,128)(2,1)S(1)}, u32[]{:S(2)}, u32[]{:S(2)}) %collective-permute-start.20) | collective-permute-done | bytes 1572896 | tf_op jit(solution)/shard_map/ppermute | solution.py:169
  480.4 3.3 add_convert_fusion
  483.8 1.1 copy-done.8
  484.8 5.7 all-to-all-start.6
  491.0 3.1 add_convert_fusion.4
  494.7 36.5 %collective-permute-done.14 = bf16[48,128,128]{2,1,0:T(8,128)(2,1)} collective-permute-done((bf16[48,128,128]{2,1,0:T(8,128)(2,1)}, bf16[48,128,128]{2,1,0:T(8,128)(2,1)}, u32[]{:S(2)}, u32[]{:S(2)}) %collective-permute-start.14) | collective-permute-done | bytes 1572896 | tf_op jit(solution)/shard_map/ppermute | solution.py:169
  531.2 4.0 add_convert_fusion.3
  535.2 7.7 %all-to-all-done.6 = bf16[8,6,128,128]{3,2,1,0:T(8,128)(2,1)S(1)} async-done(((bf16[8,6,128,128]{3,2,1,0:T(8,128)(2,1)}), bf16[8,6,128,128]{3,2,1,0:T(8,128)(2,1)S(1)}, u32[]{:S(2)}, u32[]{:S(2)}) %all-to-all-start.6) | async-done | bytes 1572896 | tf_op jit(solution)/shard_map/all_to_all | solution.py:176
  542.9 4.3 all-to-all-start.4
  547.3 0.8 gather_fusion.6
  548.0 0.8 gather_fusion.4
  549.6 5.0 fusion.21
  554.6 5.0 fusion.20
  559.6 3.1 pad_maximum_fusion.1
  562.7 2.6 gather_fusion.7
  565.6 26.3 %all-to-all-done.4 = bf16[8,6,128,128]{3,2,1,0:T(8,128)(2,1)} async-done(((bf16[8,6,128,128]{3,2,1,0:T(8,128)(2,1)}), bf16[8,6,128,128]{3,2,1,0:T(8,128)(2,1)}, u32[]{:S(2)}, u32[]{:S(2)}) %all-to-all-start.4) | async-done | bytes 1572896 | tf_op jit(solution)/shard_map/all_to_all | solution.py:176
  592.0 3.6 pad_maximum_fusion
  595.6 3.7 gather_fusion.5
  599.9 29.5 %collective-permute-done.27.refs_5_ = bf16[42,128,128]{2,1,0:T(8,128)(2,1)} collective-permute-done((bf16[42,128,128]{2,1,0:T(8,128)(2,1)}, bf16[42,128,128]{2,1,0:T(8,128)(2,1)}, u32[]{:S(2)}, u32[]{:S(2)}) %collective-permute-start.27) | collective-permute-done | bytes 1376288 | tf_op jit(solution)/shard_map/ppermute | solution.py:169
  629.5 1.1 copy.31
  630.6 0.9 copy.32
  631.5 1.4 collective-permute-done.29.refs_7_
  632.9 14.1 %collect.1 = f32[2,168,128,128]{3,2,1,0:T(8,128)} custom-call(s32[336]{0:T(512)S(1)} %pad_add_fusion.slots, bf16[42,128,128]{2,1,0:T(8,128)(2,1)S(1)} %gather_fusion.7, bf16[42,128,128]{2,1,0:T(8,128)(2,1)S(1)} %collective-permute-done.24.refs_1_, bf16[42,128,128]{2,1,0:T(8,128)(2,1)} %collective-permute-done.25.refs_2_, ...), custom_call_target="tpu_custom_call" | custom-call | tf_op jit(solution)/shard_map/collect/pallas_call | solution.py:316
  (136 shorter events, 12.8 us)
Async XLA Ops:
  15.3 38.6 %all-to-all-start.2 = ((bf16[8,5,128,128]{3,2,1,0:T(8,128)(2,1)}), bf16[8,5,128,128]{3,2,1,0:T(8,128)(2,1)S(1)}, u32[]{:S(2)}, u32[]{:S(2)}) async-start(bf16[8,5,128,128]{3,2,1,0:T(8,128)(2,1)} %bitcast.11), calls=%async_computation.2 | async-start | bytes 2621440 | tf_op jit(solution)/shard_map/all_to_all | solution.py:176
  54.0 220.9 %copy-start.1 = (bf16[8,5,128,128]{3,2,1,0:T(8,128)(2,1)}, bf16[8,5,128,128]{3,2,1,0:T(8,128)(2,1)S(1)}, u32[]{:S(2)}) copy-start(bf16[8,5,128,128]{3,2,1,0:T(8,128)(2,1)S(1)} %all-to-all-done.2) | copy-start | bytes 3932164
  54.0 40.9 %all-to-all-start.1 = ((bf16[8,6,128,128]{3,2,1,0:T(8,128)(2,1)}), bf16[8,6,128,128]{3,2,1,0:T(8,128)(2,1)}, u32[]{:S(2)}, u32[]{:S(2)}) async-start(bf16[8,6,128,128]{3,2,1,0:T(8,128)(2,1)} %bitcast.9), calls=%async_computation.1 | async-start | bytes 3145728 | tf_op jit(solution)/shard_map/all_to_all | solution.py:176
  94.9 4.5 copy-start.14
  94.9 49.5 %all-to-all-start.3 = ((bf16[8,6,128,128]{3,2,1,0:T(8,128)(2,1)}), bf16[8,6,128,128]{3,2,1,0:T(8,128)(2,1)}, u32[]{:S(2)}, u32[]{:S(2)}) async-start(bf16[8,6,128,128]{3,2,1,0:T(8,128)(2,1)} %bitcast.13), calls=%async_computation.3 | async-start | bytes 3145728 | tf_op jit(solution)/shard_map/all_to_all | solution.py:176
  99.4 88.7 %all-gather.2.cloned.1.call-start = ((), (), s32[]{:S(2)}) async-start(), calls=%async_computation.9 | async-start | bytes 2359296 | tf_op jit(solution)/shard_map/all_gather | solution.py:198
  144.4 48.3 %all-to-all-start = ((bf16[8,5,128,128]{3,2,1,0:T(8,128)(2,1)}), bf16[8,5,128,128]{3,2,1,0:T(8,128)(2,1)S(1)}, u32[]{:S(2)}, u32[]{:S(2)}) async-start(bf16[8,5,128,128]{3,2,1,0:T(8,128)(2,1)} %bitcast.109), calls=%async_computation | async-start | bytes 2621440 | tf_op jit(solution)/shard_map/all_to_all | solution.py:176
  148.3 4.9 copy-start.15
  148.3 31.9 %collective-permute-start.3 = (bf16[40,128,128]{2,1,0:T(8,128)(2,1)S(1)}, bf16[40,128,128]{2,1,0:T(8,128)(2,1)}, u32[]{:S(2)}, u32[]{:S(2)}) collective-permute-start(bf16[40,128,128]{2,1,0:T(8,128)(2,1)S(1)} %bitcast.99), channel_id=1, source_target_pairs={{0,16},{8,24},{16,0},{24,8},{1,17},{9,25},{17,1},{25,9},{2,18},{10... | collective-permute-start | bytes 3932168 | tf_op jit(solution)/shard_map/ppermute | solution.py:169
  149.9 42.8 %collective-permute-start.4 = (bf16[40,128,128]{2,1,0:T(8,128)(2,1)S(1)}, bf16[40,128,128]{2,1,0:T(8,128)(2,1)}, u32[]{:S(2)}, u32[]{:S(2)}) collective-permute-start(bf16[40,128,128]{2,1,0:T(8,128)(2,1)S(1)} %bitcast.100), channel_id=1, source_target_pairs={{0,8},{8,0},{16,24},{24,16},{1,9},{9,1},{17,25},{25,17},{2,10},{10... | collective-permute-start | bytes 3932168 | tf_op jit(solution)/shard_map/ppermute | solution.py:163
  150.9 63.0 %collective-permute-start = (bf16[48,128,128]{2,1,0:T(8,128)(2,1)}, bf16[48,128,128]{2,1,0:T(8,128)(2,1)}, u32[]{:S(2)}, u32[]{:S(2)}) collective-permute-start(bf16[48,128,128]{2,1,0:T(8,128)(2,1)} %bitcast.10.refs_0_), channel_id=1, source_target_pairs={{0,16},{8,24},{16,0},{24,8},{1,17},{9,25},{17,1},{25,9},{2,18},{10... | collective-permute-start | bytes 4718600 | tf_op jit(solution)/shard_map/ppermute | solution.py:169
  151.5 62.4 %collective-permute-start.1 = (bf16[48,128,128]{2,1,0:T(8,128)(2,1)}, bf16[48,128,128]{2,1,0:T(8,128)(2,1)}, u32[]{:S(2)}, u32[]{:S(2)}) collective-permute-start(bf16[48,128,128]{2,1,0:T(8,128)(2,1)} %bitcast.10.refs_0_), channel_id=1, source_target_pairs={{0,8},{8,0},{16,24},{24,16},{1,9},{9,1},{17,25},{25,17},{2,10},{10... | collective-permute-start | bytes 4718600 | tf_op jit(solution)/shard_map/ppermute | solution.py:163
  151.7 95.9 %collective-permute-start.6 = (bf16[48,128,128]{2,1,0:T(8,128)(2,1)}, bf16[48,128,128]{2,1,0:T(8,128)(2,1)}, u32[]{:S(2)}, u32[]{:S(2)}) collective-permute-start(bf16[48,128,128]{2,1,0:T(8,128)(2,1)} %bitcast.14.refs_0_.refs_1_), channel_id=1, source_target_pairs={{0,16},{8,24},{16,0},{24,8},{1,17},{9,25},{17,1},{25,9},{2,18},{10... | collective-permute-start | bytes 4718600 | tf_op jit(solution)/shard_map/ppermute | solution.py:169
  180.2 67.4 %collective-permute-start.5 = (bf16[40,128,128]{2,1,0:T(8,128)(2,1)}, bf16[40,128,128]{2,1,0:T(8,128)(2,1)}, u32[]{:S(2)}, u32[]{:S(2)}) collective-permute-start(bf16[40,128,128]{2,1,0:T(8,128)(2,1)} %collective-permute-done.3.refs_5_), channel_id=1, source_target_pairs={{0,8},{8,0},{16,24},{24,16},{1,9},{9,1},{17,25},{25,17},{2,10},{10... | collective-permute-start | bytes 3932168 | tf_op jit(solution)/shard_map/ppermute | solution.py:163
  192.7 106.4 %copy-start = (bf16[8,5,128,128]{3,2,1,0:T(8,128)(2,1)}, bf16[8,5,128,128]{3,2,1,0:T(8,128)(2,1)S(1)}, u32[]{:S(2)}) copy-start(bf16[8,5,128,128]{3,2,1,0:T(8,128)(2,1)S(1)} %all-to-all-done) | copy-start | bytes 3932164
  192.7 81.5 %collective-permute-start.9 = (bf16[40,128,128]{2,1,0:T(8,128)(2,1)S(1)}, bf16[40,128,128]{2,1,0:T(8,128)(2,1)S(1)}, u32[]{:S(2)}, u32[]{:S(2)}) collective-permute-start(bf16[40,128,128]{2,1,0:T(8,128)(2,1)S(1)} %bitcast.95), channel_id=1, source_target_pairs={{0,16},{8,24},{16,0},{24,8},{1,17},{9,25},{17,1},{25,9},{2,18},{10... | collective-permute-start | bytes 3932168 | tf_op jit(solution)/shard_map/ppermute | solution.py:169
  213.9 61.0 %collective-permute-start.2 = (bf16[48,128,128]{2,1,0:T(8,128)(2,1)}, bf16[48,128,128]{2,1,0:T(8,128)(2,1)S(1)}, u32[]{:S(2)}, u32[]{:S(2)}) collective-permute-start(bf16[48,128,128]{2,1,0:T(8,128)(2,1)} %collective-permute-done.refs_1_), channel_id=1, source_target_pairs={{0,8},{8,0},{16,24},{24,16},{1,9},{9,1},{17,25},{25,17},{2,10},{10... | collective-permute-start | bytes 4718600 | tf_op jit(solution)/shard_map/ppermute | solution.py:163
  213.9 85.1 %collective-permute-start.7 = (bf16[48,128,128]{2,1,0:T(8,128)(2,1)}, bf16[48,128,128]{2,1,0:T(8,128)(2,1)S(1)}, u32[]{:S(2)}, u32[]{:S(2)}) collective-permute-start(bf16[48,128,128]{2,1,0:T(8,128)(2,1)} %bitcast.14.refs_0_.refs_1_), channel_id=1, source_target_pairs={{0,8},{8,0},{16,24},{24,16},{1,9},{9,1},{17,25},{25,17},{2,10},{10... | collective-permute-start | bytes 4718600 | tf_op jit(solution)/shard_map/ppermute | solution.py:163
  247.6 51.4 %collective-permute-start.8 = (bf16[48,128,128]{2,1,0:T(8,128)(2,1)}, bf16[48,128,128]{2,1,0:T(8,128)(2,1)S(1)}, u32[]{:S(2)}, u32[]{:S(2)}) collective-permute-start(bf16[48,128,128]{2,1,0:T(8,128)(2,1)} %collective-permute-done.6.refs_1_.refs_2_), channel_id=1, source_target_pairs={{0,8},{8,0},{16,24},{24,16},{1,9},{9,1},{17,25},{25,17},{2,10},{10... | collective-permute-start | bytes 4718600 | tf_op jit(solution)/shard_map/ppermute | solution.py:163
  247.6 51.4 %collective-permute-start.10 = (bf16[40,128,128]{2,1,0:T(8,128)(2,1)S(1)}, bf16[40,128,128]{2,1,0:T(8,128)(2,1)S(1)}, u32[]{:S(2)}, u32[]{:S(2)}) collective-permute-start(bf16[40,128,128]{2,1,0:T(8,128)(2,1)S(1)} %bitcast.96), channel_id=1, source_target_pairs={{0,8},{8,0},{16,24},{24,16},{1,9},{9,1},{17,25},{25,17},{2,10},{10... | collective-permute-start | bytes 3932168 | tf_op jit(solution)/shard_map/ppermute | solution.py:163
  274.1 24.9 %copy-start.2 = (bf16[40,128,128]{2,1,0:T(8,128)(2,1)}, bf16[40,128,128]{2,1,0:T(8,128)(2,1)S(1)}, u32[]{:S(2)}) copy-start(bf16[40,128,128]{2,1,0:T(8,128)(2,1)S(1)} %collective-permute-done.9.refs_5_.refs_6_) | copy-start | bytes 3932164
  274.2 24.9 %collective-permute-start.11 = (bf16[40,128,128]{2,1,0:T(8,128)(2,1)S(1)}, bf16[40,128,128]{2,1,0:T(8,128)(2,1)}, u32[]{:S(2)}, u32[]{:S(2)}) collective-permute-start(bf16[40,128,128]{2,1,0:T(8,128)(2,1)S(1)} %collective-permute-done.9.refs_5_.refs_6_), channel_id=1, source_target_pairs={{0,8},{8,0},{16,24},{24,16},{1,9},{9,1},{17,25},{25,17},{2,10},{10... | collective-permute-start | bytes 3932168 | tf_op jit(solution)/shard_map/ppermute | solution.py:163
  274.9 1.2 copy-start.7
  299.0 1.7 copy-start.5
  299.0 14.0 %copy-start.3 = (bf16[40,128,128]{2,1,0:T(8,128)(2,1)}, bf16[40,128,128]{2,1,0:T(8,128)(2,1)S(1)}, u32[]{:S(2)}) copy-start(bf16[40,128,128]{2,1,0:T(8,128)(2,1)S(1)} %collective-permute-done.10.refs_6_.refs_7_) | copy-start | bytes 3932164
  299.0 1.6 copy-start.6
  300.6 12.4 %copy-start.4 = (f32[128,3584]{1,0:T(8,128)S(1)}, f32[128,3584]{1,0:T(8,128)}, u32[]{:S(2)}) copy-start(f32[128,3584]{1,0:T(8,128)} %project.2) | copy-start | bytes 5505028
  300.6 12.4 %copy-start.13 = (bf16[128,3584]{1,0:T(8,128)(2,1)S(1)}, bf16[128,3584]{1,0:T(8,128)(2,1)}, u32[]{:S(2)}) copy-start(bf16[128,3584]{1,0:T(8,128)(2,1)} %param.6) | copy-start | bytes 2752516
  348.8 3.3 collective-permute-start.22
  349.3 24.7 %collective-permute-start.21 = (bf16[40,128,128]{2,1,0:T(8,128)(2,1)}, bf16[40,128,128]{2,1,0:T(8,128)(2,1)S(1)}, u32[]{:S(2)}, u32[]{:S(2)}) collective-permute-start(bf16[40,128,128]{2,1,0:T(8,128)(2,1)} %get-tuple-element.51), channel_id=1, source_target_pairs={{0,8},{8,0},{16,24},{24,16},{1,9},{9,1},{17,25},{25,17},{2,10},{10... | collective-permute-start | bytes 3932168 | tf_op jit(solution)/shard_map/ppermute | solution.py:163
  352.6 31.1 %collective-permute-start.23 = (bf16[40,128,128]{2,1,0:T(8,128)(2,1)S(1)}, bf16[40,128,128]{2,1,0:T(8,128)(2,1)S(1)}, u32[]{:S(2)}, u32[]{:S(2)}) collective-permute-start(bf16[40,128,128]{2,1,0:T(8,128)(2,1)S(1)} %add_convert_fusion.7), channel_id=1, source_target_pairs={{0,16},{8,24},{16,0},{24,8},{1,17},{9,25},{17,1},{25,9},{2,18},{10... | collective-permute-start | bytes 3932168 | tf_op jit(solution)/shard_map/ppermute | solution.py:169
  373.9 27.9 %collective-permute-start.16 = (bf16[40,128,128]{2,1,0:T(8,128)(2,1)}, bf16[40,128,128]{2,1,0:T(8,128)(2,1)}, u32[]{:S(2)}, u32[]{:S(2)}) collective-permute-start(bf16[40,128,128]{2,1,0:T(8,128)(2,1)} %get-tuple-element.43), channel_id=1, source_target_pairs={{0,8},{8,0},{16,24},{24,16},{1,9},{9,1},{17,25},{25,17},{2,10},{10... | collective-permute-start | bytes 3932168 | tf_op jit(solution)/shard_map/ppermute | solution.py:163
  385.4 51.0 %all-to-all-start.7 = ((bf16[8,5,128,128]{3,2,1,0:T(8,128)(2,1)}), bf16[8,5,128,128]{3,2,1,0:T(8,128)(2,1)}, u32[]{:S(2)}, u32[]{:S(2)}) async-start(bf16[8,5,128,128]{3,2,1,0:T(8,128)(2,1)} %bitcast.108), calls=%async_computation.8 | async-start | bytes 2621440 | tf_op jit(solution)/shard_map/all_to_all | solution.py:176
  401.6 3.2 collective-permute-start.15
  403.6 31.1 %collective-permute-start.17 = (bf16[40,128,128]{2,1,0:T(8,128)(2,1)S(1)}, bf16[40,128,128]{2,1,0:T(8,128)(2,1)S(1)}, u32[]{:S(2)}, u32[]{:S(2)}) collective-permute-start(bf16[40,128,128]{2,1,0:T(8,128)(2,1)S(1)} %add_convert_fusion.10), channel_id=1, source_target_pairs={{0,16},{8,24},{16,0},{24,8},{1,17},{9,25},{17,1},{25,9},{2,18},{10... | collective-permute-start | bytes 3932168 | tf_op jit(solution)/shard_map/ppermute | solution.py:169
  404.2 38.4 %collective-permute-start.19 = (bf16[48,128,128]{2,1,0:T(8,128)(2,1)}, bf16[48,128,128]{2,1,0:T(8,128)(2,1)}, u32[]{:S(2)}, u32[]{:S(2)}) collective-permute-start(bf16[48,128,128]{2,1,0:T(8,128)(2,1)} %get-tuple-element.49), channel_id=1, source_target_pairs={{0,8},{8,0},{16,24},{24,16},{1,9},{9,1},{17,25},{25,17},{2,10},{10... | collective-permute-start | bytes 4718600 | tf_op jit(solution)/shard_map/ppermute | solution.py:163
  404.2 41.0 %collective-permute-start.18 = (bf16[48,128,128]{2,1,0:T(8,128)(2,1)}, bf16[48,128,128]{2,1,0:T(8,128)(2,1)}, u32[]{:S(2)}, u32[]{:S(2)}) collective-permute-start(bf16[48,128,128]{2,1,0:T(8,128)(2,1)} %get-tuple-element.47), channel_id=1, source_target_pairs={{0,8},{8,0},{16,24},{24,16},{1,9},{9,1},{17,25},{25,17},{2,10},{10... | collective-permute-start | bytes 4718600 | tf_op jit(solution)/shard_map/ppermute | solution.py:163
  436.4 6.1 copy-start.12
  436.4 47.4 %all-to-all-start.5 = ((bf16[8,5,128,128]{3,2,1,0:T(8,128)(2,1)}), bf16[8,5,128,128]{3,2,1,0:T(8,128)(2,1)S(1)}, u32[]{:S(2)}, u32[]{:S(2)}) async-start(bf16[8,5,128,128]{3,2,1,0:T(8,128)(2,1)} %bitcast.17), calls=%async_computation.5 | async-start | bytes 2621440 | tf_op jit(solution)/shard_map/all_to_all | solution.py:176
  442.5 37.9 %copy-start.10 = (bf16[48,128,128]{2,1,0:T(8,128)(2,1)S(1)}, bf16[48,128,128]{2,1,0:T(8,128)(2,1)}, u32[]{:S(2)}) copy-start(bf16[48,128,128]{2,1,0:T(8,128)(2,1)} %get-tuple-element.46) | copy-start | bytes 4718596
  444.6 35.8 %collective-permute-start.20 = (bf16[48,128,128]{2,1,0:T(8,128)(2,1)S(1)}, bf16[48,128,128]{2,1,0:T(8,128)(2,1)S(1)}, u32[]{:S(2)}, u32[]{:S(2)}) collective-permute-start(bf16[48,128,128]{2,1,0:T(8,128)(2,1)S(1)} %add_convert_fusion.1), channel_id=1, source_target_pairs={{0,16},{8,24},{16,0},{24,8},{1,17},{9,25},{17,1},{25,9},{2,18},{10... | collective-permute-start | bytes 4718600 | tf_op jit(solution)/shard_map/ppermute | solution.py:169
  445.2 45.7 %collective-permute-start.13 = (bf16[48,128,128]{2,1,0:T(8,128)(2,1)}, bf16[48,128,128]{2,1,0:T(8,128)(2,1)}, u32[]{:S(2)}, u32[]{:S(2)}) collective-permute-start(bf16[48,128,128]{2,1,0:T(8,128)(2,1)} %get-tuple-element.39), channel_id=1, source_target_pairs={{0,8},{8,0},{16,24},{24,16},{1,9},{9,1},{17,25},{25,17},{2,10},{10... | collective-permute-start | bytes 4718600 | tf_op jit(solution)/shard_map/ppermute | solution.py:163
  483.8 1.1 copy-start.8
  483.8 7.2 %copy-start.11 = (bf16[48,128,128]{2,1,0:T(8,128)(2,1)S(1)}, bf16[48,128,128]{2,1,0:T(8,128)(2,1)}, u32[]{:S(2)}) copy-start(bf16[48,128,128]{2,1,0:T(8,128)(2,1)} %get-tuple-element.38) | copy-start | bytes 4718596
  484.8 58.1 %all-to-all-start.6 = ((bf16[8,6,128,128]{3,2,1,0:T(8,128)(2,1)}), bf16[8,6,128,128]{3,2,1,0:T(8,128)(2,1)S(1)}, u32[]{:S(2)}, u32[]{:S(2)}) async-start(bf16[8,6,128,128]{3,2,1,0:T(8,128)(2,1)} %bitcast.35), calls=%async_computation.7 | async-start | bytes 3145728 | tf_op jit(solution)/shard_map/all_to_all | solution.py:176
  490.6 108.8 %reduce-scatter.2.cloned.1.call-start = ((), (), s32[]{:S(2)}) async-start(), calls=%async_computation.10 | async-start | bytes 2359296 | tf_op jit(solution)/shard_map/reduce_scatter | solution.py:309
  490.9 3.8 collective-permute-start.12
  494.1 37.1 %copy-start.9 = (bf16[48,128,128]{2,1,0:T(8,128)(2,1)S(1)}, bf16[48,128,128]{2,1,0:T(8,128)(2,1)}, u32[]{:S(2)}) copy-start(bf16[48,128,128]{2,1,0:T(8,128)(2,1)} %get-tuple-element.36) | copy-start | bytes 4718596
  494.1 37.1 %collective-permute-start.14 = (bf16[48,128,128]{2,1,0:T(8,128)(2,1)}, bf16[48,128,128]{2,1,0:T(8,128)(2,1)}, u32[]{:S(2)}, u32[]{:S(2)}) collective-permute-start(bf16[48,128,128]{2,1,0:T(8,128)(2,1)} %add_convert_fusion.4), channel_id=1, source_target_pairs={{0,16},{8,24},{16,0},{24,8},{1,17},{9,25},{17,1},{25,9},{2,18},{10... | collective-permute-start | bytes 4718600 | tf_op jit(solution)/shard_map/ppermute | solution.py:169
  542.9 49.1 %all-to-all-start.4 = ((bf16[8,6,128,128]{3,2,1,0:T(8,128)(2,1)}), bf16[8,6,128,128]{3,2,1,0:T(8,128)(2,1)}, u32[]{:S(2)}, u32[]{:S(2)}) async-start(bf16[8,6,128,128]{3,2,1,0:T(8,128)(2,1)} %bitcast.15), calls=%async_computation.4 | async-start | bytes 3145728 | tf_op jit(solution)/shard_map/all_to_all | solution.py:176
  565.4 34.5 %collective-permute-start.24 = (bf16[42,128,128]{2,1,0:T(8,128)(2,1)S(1)}, bf16[42,128,128]{2,1,0:T(8,128)(2,1)S(1)}, u32[]{:S(2)}, u32[]{:S(2)}) collective-permute-start(bf16[42,128,128]{2,1,0:T(8,128)(2,1)S(1)} %gather_fusion.7), channel_id=1, source_target_pairs={{0,16},{8,24},{16,0},{24,8},{1,17},{9,25},{17,1},{25,9},{2,18},{10... | collective-permute-start | bytes 4128776 | tf_op jit(solution)/shard_map/ppermute | solution.py:169
  599.3 30.1 %collective-permute-start.27 = (bf16[42,128,128]{2,1,0:T(8,128)(2,1)}, bf16[42,128,128]{2,1,0:T(8,128)(2,1)}, u32[]{:S(2)}, u32[]{:S(2)}) collective-permute-start(bf16[42,128,128]{2,1,0:T(8,128)(2,1)} %gather_fusion.5), channel_id=1, source_target_pairs={{0,16},{8,24},{16,0},{24,8},{1,17},{9,25},{17,1},{25,9},{2,18},{10... | collective-permute-start | bytes 4128776 | tf_op jit(solution)/shard_map/ppermute | solution.py:169
  599.3 32.2 %collective-permute-start.25 = (bf16[42,128,128]{2,1,0:T(8,128)(2,1)S(1)}, bf16[42,128,128]{2,1,0:T(8,128)(2,1)}, u32[]{:S(2)}, u32[]{:S(2)}) collective-permute-start(bf16[42,128,128]{2,1,0:T(8,128)(2,1)S(1)} %gather_fusion.7), channel_id=1, source_target_pairs={{0,8},{8,0},{16,24},{24,16},{1,9},{9,1},{17,25},{25,17},{2,10},{10... | collective-permute-start | bytes 4128776 | tf_op jit(solution)/shard_map/ppermute | solution.py:163
  599.3 32.2 %collective-permute-start.28 = (bf16[42,128,128]{2,1,0:T(8,128)(2,1)}, bf16[42,128,128]{2,1,0:T(8,128)(2,1)}, u32[]{:S(2)}, u32[]{:S(2)}) collective-permute-start(bf16[42,128,128]{2,1,0:T(8,128)(2,1)} %gather_fusion.5), channel_id=1, source_target_pairs={{0,8},{8,0},{16,24},{24,16},{1,9},{9,1},{17,25},{25,17},{2,10},{10... | collective-permute-start | bytes 4128776 | tf_op jit(solution)/shard_map/ppermute | solution.py:163
  599.8 31.7 %collective-permute-start.26 = (bf16[42,128,128]{2,1,0:T(8,128)(2,1)S(1)}, bf16[42,128,128]{2,1,0:T(8,128)(2,1)}, u32[]{:S(2)}, u32[]{:S(2)}) collective-permute-start(bf16[42,128,128]{2,1,0:T(8,128)(2,1)S(1)} %collective-permute-done.24.refs_1_), channel_id=1, source_target_pairs={{0,8},{8,0},{16,24},{24,16},{1,9},{9,1},{17,25},{25,17},{2,10},{10... | collective-permute-start | bytes 4128776 | tf_op jit(solution)/shard_map/ppermute | solution.py:163
  629.4 3.5 collective-permute-start.29
Sparse Core Ops, SparseCore 0:
  102.9 85.1 all-gather.1
  494.9 94.8 reduce-scatter.1

commit v3 on v2

--- a/solution.py
+++ b/solution.py
@@ -46,11 +46,11 @@
     lax.fori_loop(0, panels, panel_step, 0)
 
 
-def backward_kernel(first, count, slots, rows, steps, tokt_ref, grad_ref, *refs):
+def backward_kernel(first, count, out_count, slots, targets, rows, steps, tokt_ref, grad_ref, *refs):
     prior = () if first else refs[:1]
     refs = refs[len(prior) :]
-    pieces, terms_out, outs = refs[:count], refs[count], refs[count + 1 : 2 * count + 1]
-    buf, grads, sems = refs[2 * count + 1 : 2 * count + 4]
+    pieces, terms_out, refs = refs[:count], refs[count], refs[count + 1 :]
+    outs, (buf, grads, sems) = refs[:out_count], refs[out_count : out_count + 3]
     terms_ref = terms_out if first else refs[-1]
     load_pieces(pieces, buf, sems)
     size = tokt_ref.shape[1]
@@ -64,6 +64,7 @@
             base = p * KHEAVY + t * KLIGHT
             row = [rows[base + i] for i in range(KLIGHT)]
             slot = [slots[base + i] for i in range(KLIGHT)]
+            target = [targets[base + i] for i in range(KLIGHT)]
             weight = jnp.concatenate([buf[s] for s in slot], axis=0)
             back = lax.dot_general(
                 column, weight, (((1,), (1,)), ((), ())), preferred_element_type=jnp.float32
@@ -73,7 +74,7 @@
             before = [terms_ref[r] for r in row]
             for i in range(KLIGHT):
                 terms_ref[row[i]] = before[i] + back[:, i * size : (i + 1) * size]
-                grads[slot[i]] = outer[i * size : (i + 1) * size]
+                grads[target[i]] = outer[i * size : (i + 1) * size]
             return inner
 
         return lax.fori_loop(0, steps[0], group, carry)
@@ -134,6 +135,7 @@
     share = (capacity + groups - 1) // groups
     parts = [(0, (share + 1) // 2), ((share + 1) // 2, share // 2)]
     parts = [(low, count) for low, count in parts if count]
+    undivided = [(0, share)]
     packed = (owned + groups - 1) // groups
     slot_count = groups * members * share
     smem = pl.BlockSpec(memory_space=pltpu.SMEM)
@@ -150,9 +152,9 @@
     def skipped(start, sender):
         return (start - sender + groups - 1) // groups
 
-    def place(piece, partner, q):
+    def place(piece, partner, q, cuts):
         found, base = 0, 0
-        for low, count in parts:
+        for low, count in cuts:
             here = base + (piece * members + partner) * count + q - low
             found = jnp.where(q >= low, here, found)
             base += groups * members * count
@@ -168,9 +170,11 @@
         ]
         return lax.ppermute(x, "dp", pairs)
 
+    def both(mine):
+        return mine + [swap_cores(piece) for piece in mine]
+
     def spread(x):
-        mine = [x] + [shift_y(x, s) for s in range(1, lanes)]
-        return mine + [swap_cores(piece) for piece in mine]
+        return both([x] + [shift_y(x, s) for s in range(1, lanes)])
 
     def exchange(x):
         swapped = lax.all_to_all(
@@ -186,14 +190,6 @@
     start = jnp.sum((my_holder[:, None, :] < member_ids[None, :, None]).astype(ints), axis=2)
     lead = skipped(start, group_id)
     flat_tiles = tiles.reshape(2 * owned, size, size)
-    landed = []
-    for m in range(2):
-        for low, count in parts:
-            source = (lead[m][:, None] + low + jnp.arange(count, dtype=ints)[None, :]) * groups
-            source = jnp.minimum(source + group_id, owned - 1) + m * owned
-            picked = jnp.take(flat_tiles, source.reshape(-1), axis=0, mode="clip")
-            landed.append(exchange(picked))
-
     blocks = jnp.transpose(tokens.reshape(tok_rows, local_blocks, size), (1, 0, 2))
     tok = lax.all_gather(blocks, "mp", axis=0, tiled=True)
     tokt = jnp.transpose(tok, (0, 2, 1))
@@ -201,7 +197,10 @@
     first = jnp.sum((holder_all < myself).astype(ints), axis=2)[:, :, None]
     owner_tile = tile_ids[None, None, :]
     q_all = owner_tile // groups - skipped(first, owner_tile % groups)
-    slot_all = place(piece_of(owner_tile), member_ids[None, :, None], q_all).reshape(2, -1)
+    slot_all, target_all = [
+        place(piece_of(owner_tile), member_ids[None, :, None], q_all, cuts).reshape(2, -1)
+        for cuts in (parts, undivided)
+    ]
     local_cols = tile_cols - myself * panels
     mask = local_cols[:, None, :] == jnp.arange(panels, dtype=ints)[None, :, None]
     listed = jnp.arange(tile_cols.shape[1])
@@ -213,24 +212,24 @@
         rank[:, :, None, :] == jnp.arange(KHEAVY, dtype=ints)[None, None, :, None]
     )
     slots = jnp.sum(jnp.where(chosen, slot_all[:, None, None, :], 0), axis=3).reshape(2, -1)
+    targets = jnp.sum(jnp.where(chosen, target_all[:, None, None, :], 0), axis=3).reshape(2, -1)
     rows = jnp.sum(jnp.where(chosen, tile_rows[:, None, None, :], 0), axis=3).reshape(2, -1)
     steps = jnp.sum(mask[:, 0, :].astype(ints), axis=1) // KLIGHT
 
-    landed[-1], tok, tokt, slots, rows, steps = lax.optimization_barrier(
-        (landed[-1], tok, tokt, slots, rows, steps)
-    )
     per_matrix = len(parts)
-    arrived = [
-        sum([spread(x) for x in landed[m * per_matrix : (m + 1) * per_matrix]], [])
-        for m in range(2)
-    ]
     piece_count = per_matrix * groups
-
     slot_bytes = slot_count * size * size * 2
     flops = 2 * panels * KHEAVY * size**2 * tok_rows
     tile_buf = pltpu.VMEM((slot_count, size, size), jnp.bfloat16)
     piece_sems = pltpu.SemaphoreType.DMA((piece_count,))
     params = pltpu.CompilerParams(vmem_limit_bytes=VMEM_BYTES)
+
+    def send(m, low, count, after):
+        source = (lead[m][:, None] + low + jnp.arange(count, dtype=ints)[None, :]) * groups
+        source = jnp.minimum(source + group_id, owned - 1) + m * owned
+        picked = jnp.take(flat_tiles, source.reshape(-1), axis=0, mode="clip")
+        picked, after = lax.optimization_barrier((picked, after))
+        return exchange(picked), after
 
     def project(m):
         return pl.pallas_call(
@@ -246,7 +245,23 @@
             name="project",
         )(slots[m], rows[m], steps[m : m + 1], tok, *arrived[m])
 
-    gate_pre, up_pre = project(0), project(1)
+    stages = [(m, low, count) for m in range(2) for low, count in parts]
+    shifted = []
+    for i, stage in enumerate(stages):
+        last = i == len(stages) - 1
+        ready = shifted[i - 2] if i >= 2 else []
+        tables = (tok, tokt, slots, targets, rows, steps) if last else ()
+        landed, (ready, tables) = send(*stage, (ready, tables))
+        if i >= 2:
+            shifted[i - 2] = ready
+        if last:
+            tok, tokt, slots, targets, rows, steps = tables
+            arrived = [sum([both(x) for x in shifted[:per_matrix]], [])]
+            gate_pre = project(0)
+            landed, gate_pre = lax.optimization_barrier((landed, gate_pre))
+        shifted.append([landed] + [shift_y(landed, s) for s in range(1, lanes)])
+    arrived.append(sum([both(x) for x in shifted[per_matrix:]], []))
+    up_pre = project(1)
     sigmoid_gate = jax.nn.sigmoid(gate_pre)
     hidden = (gate_pre * sigmoid_gate * up_pre).astype(jnp.bfloat16)
     upstream = cotangent.astype(jnp.float32)
@@ -259,53 +274,50 @@
 
     def pull_back(m, grad, prior):
         begin = not prior
-        piece_shapes = [jax.ShapeDtypeStruct(x.shape, jnp.bfloat16) for x in arrived[m]]
+        piece_shape = jax.ShapeDtypeStruct((members * share, size, size), jnp.bfloat16)
         terms_type = jnp.float32 if begin else jnp.bfloat16
         scratch = [tile_buf, tile_buf, piece_sems]
         results = pl.pallas_call(
-            functools.partial(backward_kernel, begin, piece_count),
-            out_shape=[jax.ShapeDtypeStruct(terms_shape, terms_type)] + piece_shapes,
-            in_specs=[smem, smem, smem] + [vmem] * (2 + len(prior)) + [anywhere] * piece_count,
-            out_specs=[vmem] + [anywhere] * piece_count,
+            functools.partial(backward_kernel, begin, piece_count, groups),
+            out_shape=[jax.ShapeDtypeStruct(terms_shape, terms_type)] + [piece_shape] * groups,
+            in_specs=[smem] * 4 + [vmem] * (2 + len(prior)) + [anywhere] * piece_count,
+            out_specs=[vmem] + [anywhere] * groups,
             scratch_shapes=scratch if begin else scratch + [pltpu.VMEM(terms_shape, jnp.float32)],
             compiler_params=params,
             cost_estimate=pl.CostEstimate(
                 flops=2 * flops, bytes_accessed=6 * slot_bytes, transcendentals=0
             ),
             name="pull_back",
-        )(slots[m], rows[m], steps[m : m + 1], tokt, grad, *prior, *arrived[m])
+        )(slots[m], targets[m], rows[m], steps[m : m + 1], tokt, grad, *prior, *arrived[m])
         return results[0], results[1:]
 
     def add_pair(x, y):
         return x.astype(jnp.float32) + y.astype(jnp.float32)
 
-    def total_of(pieces):
-        pair = [
+    def pairs_of(pieces):
+        return [
             add_pair(pieces[s], swap_cores(pieces[lanes + s])).astype(jnp.bfloat16)
-            for s in range(lanes)
+            for s in range(1, lanes)
         ]
-        total = pair[0].astype(jnp.float32)
+
+    def total_of(pieces, pairs):
+        total = add_pair(pieces[0], swap_cores(pieces[lanes]))
         for s in range(1, lanes):
-            total = total + shift_y(pair[s], lanes - s).astype(jnp.float32)
+            total = total + shift_y(pairs[s - 1], lanes - s).astype(jnp.float32)
         return exchange(total.astype(jnp.bfloat16))
-
-    def totals_of(pieces):
-        return [total_of(pieces[i * groups : (i + 1) * groups]) for i in range(per_matrix)]
 
     def pack(m, returned):
         held = jnp.minimum(jnp.arange(packed, dtype=ints) * groups + group_id, owned - 1)
         holder = jnp.take(my_holder[m], held, mode="clip")
         q = held // groups - jnp.take(lead[m], holder, mode="clip")
-        found, base = 0, 0
-        for low, count in parts:
-            found = jnp.where(q >= low, base + holder * count + q - low, found)
-            base += members * count
-        return jnp.take(jnp.concatenate(returned, axis=0), found, axis=0, mode="clip")
+        return jnp.take(returned, holder * share + q, axis=0, mode="clip")
 
     gate_terms, gate_pieces = pull_back(0, gate_grad, [])
+    gate_pairs = pairs_of(gate_pieces)
+    up_grad, gate_pairs = lax.optimization_barrier((up_grad, gate_pairs))
     terms, up_pieces = pull_back(1, up_grad, [gate_terms])
-    gate_back = pack(0, totals_of(gate_pieces))
-    up_back = pack(1, totals_of(up_pieces))
+    gate_back = pack(0, total_of(gate_pieces, gate_pairs))
+    up_back = pack(1, total_of(up_pieces, pairs_of(up_pieces)))
     mine = lax.psum_scatter(terms, "mp", scatter_dimension=0, tiled=True)
     up_back, mine = lax.optimization_barrier((up_back, mine))
     home_pieces = spread(gate_back) + spread(up_back)

time: 649 us -> 613 us (0.945)
  waiting for transfers between devices: 374 us -> 345 us
  starting transfers between devices: 64.3 us -> 49.1 us
    ppermute x10 -> x8, waiting for transfers between devices: 234 us -> 182 us  [shift_y(): return lax.ppermute(x, 'dp', pairs)]
    reduce_scatter x1, waiting for transfers between devices: 0.01 us -> 23 us  [per_device(): mine = lax.psum_scatter(terms, 'mp', scatter_dimension=0, tiled=True)]
    all_to_all x8 -> x6, waiting for transfers between devices: 127 us -> 106 us  [exchange(): lax.all_to_all(x.reshape(members, -1, size, size), 'mp', split_axis=0, co...]
    all_to_all x8 -> x6, starting transfers between devices: 52.1 us -> 34.1 us  [exchange(): lax.all_to_all(x.reshape(members, -1, size, size), 'mp', split_axis=0, co...]
    ppermute x20 -> x16, waiting for transfers between devices: 4.46 us -> 15.8 us  [swap_cores(): return lax.ppermute(x, 'dp', pairs)]
    add x3, other arithmetic: 0.09 us -> 10.2 us  [the longest x2 10.1 us: pack(): return jnp.take(returned, holder * share + q, axis=0, mode='clip')]
    select_n x2 -> x0, other arithmetic: 9.96 us -> none  [pack(): found = jnp.where(q >= low, base + holder * count + q - low, found)]
    all_gather x1, waiting for transfers between devices: 7.92 us -> 17.3 us  [per_device(): tok = lax.all_gather(blocks, 'mp', axis=0, tiled=True)]
  transfers between devices with their start and end apart: 40 -> 32, of which waited for: 20 -> 18; matrix products, arithmetic and copies ran while one was open for 13% -> 14% of each run, Pallas kernels for 7% -> 7%
where the time goes in v3:
time: 613 us; the launch traced here: 612 us
  waiting for transfers between devices  345 us (56%)
  Pallas kernels  101 us (16%)
  local copies, waits for them, and re-layouts  52.2 us (9%)
  other arithmetic  50 us (8%)
  starting transfers between devices  49.1 us (8%)
  between operations  14.6 us (2%)
    ppermute x8, waiting for transfers between devices, shift_y(): return lax.ppermute(x, 'dp', pairs)  182 us
    all_to_all x6, waiting for transfers between devices, exchange(): lax.all_to_all(x.reshape(members, -1, size, size), 'mp', split_axis=0, co...  106 us
    pallas_call x2, Pallas kernels, pull_back(): pl.pallas_call(functools.partial(backward_kernel, begin, piece_count, gro...  52.1 us
    pallas_call x2, Pallas kernels, project(): pl.pallas_call(forward_kernel, out_shape=jax.ShapeDtypeStruct(cotangent.s...  34.5 us
    all_to_all x6, starting transfers between devices, exchange(): lax.all_to_all(x.reshape(members, -1, size, size), 'mp', split_axis=0, co...  34.1 us
    gather x4, local copies, waits for them, and re-layouts, send(): picked = jnp.take(flat_tiles, source.reshape(-1), axis=0, mode='clip')  24.2 us
    reduce_scatter x1, waiting for transfers between devices, per_device(): mine = lax.psum_scatter(terms, 'mp', scatter_dimension=0, tiled=True)  23 us
    reduce_sum x1, other arithmetic, per_device(): jnp.sum(jnp.where(chosen, tile_rows[:, None, None, :], 0), axis=3)  17.7 us
  transfers between devices with their start and end apart: 32, of which 18 were waited for; matrix products, arithmetic and copies ran while one was open for 14% of the time, Pallas kernels for 7%

profile of v3, /device:TPU:0, one launch (start us, length us, event | category | flops | bytes accessed | tf_op | source)
XLA Modules:
  0.0 611.9 jit_solution(4609516662014226898)
XLA Ops:
  7.2 0.7 compare_and_fusion.1
  8.0 0.7 broadcast_subtract_fusion
  9.4 6.1 gather_fusion.3
  15.5 7.3 %all-to-all-start.2 = ((bf16[8,6,128,128]{3,2,1,0:T(8,128)(2,1)}), bf16[8,6,128,128]{3,2,1,0:T(8,128)(2,1)S(1)}, u32[]{:S(2)}, u32[]{:S(2)}) async-start(bf16[8,6,128,128]{3,2,1,0:T(8,128)(2,1)} %bitcast.101), calls=%async_computation.2 | async-start | bytes 3145728 | tf_op jit(solution)/shard_map/all_to_all | solution.py:180
  22.9 6.0 gather_fusion.1
  28.9 30.8 %all-to-all-done.2 = bf16[8,6,128,128]{3,2,1,0:T(8,128)(2,1)S(1)} async-done(((bf16[8,6,128,128]{3,2,1,0:T(8,128)(2,1)}), bf16[8,6,128,128]{3,2,1,0:T(8,128)(2,1)S(1)}, u32[]{:S(2)}, u32[]{:S(2)}) %all-to-all-start.2) | async-done | bytes 1572896 | tf_op jit(solution)/shard_map/all_to_all | solution.py:180
  59.7 3.6 all-to-all-start
  63.4 1.6 collective-permute-start.1
  65.2 0.9 copy.25
  66.1 6.1 gather_fusion.2
  72.3 27.3 %collective-permute-done.1.refs_1_ = bf16[48,128,128]{2,1,0:T(8,128)(2,1)} collective-permute-done((bf16[48,128,128]{2,1,0:T(8,128)(2,1)S(1)}, bf16[48,128,128]{2,1,0:T(8,128)(2,1)}, u32[]{:S(2)}, u32[]{:S(2)}) %collective-permute-start.1) | collective-permute-done | bytes 1572896 | tf_op jit(solution)/shard_map/ppermute | solution.py:171
  99.6 3.7 all-to-all-done
  103.3 4.3 all-to-all-start.3
  109.5 1.6 collective-permute-start
  111.1 17.7 %select_reduce_fusion = (s32[2,28,12]{0,2,1:T(8,128)S(1)}, s32[2,28,12]{0,2,1:T(8,128)S(1)}, s32[2,28,12]{0,2,1:T(8,128)S(1)}) fusion(s32[2,1344]{1,0:T(2,128)S(1)} %copy-done.21, s32[2,1344]{1,0:T(2,128)S(1)} %add_select_fusion.1, s32[2,1344]{1,0:T(2,128)S(1)} %get-tuple-element.80, s32[2,28,1344]{2,0,1:T(2,128)S(1)} %copy.28, pred[2,28,1344]{2,0,1:T(4,128)(4,1)S(1)} %copy.27), kind=kLoop, calls=%fused_computation.16 | loop fusion | flops 7223328 | bytes 416640 | tf_op jit(solution)/shard_map/reduce_sum | solution.py:216
  130.1 6.1 gather_fusion
  136.3 17.3 %all-gather.2.cloned.1.call-done.tok_ref = bf16[64,128,128]{2,1,0:T(8,128)(2,1)} async-done(((bf16[8,128,128]{2,1,0:T(8,128)(2,1)}), bf16[64,128,128]{2,1,0:T(8,128)(2,1)}) %all-gather.2.cloned.1.call-update) | async-done | bytes 2097168 | tf_op jit(solution)/shard_map/all_gather | solution.py:194
  153.6 4.1 copy.26
  157.7 2.6 all-to-all-done.3
  160.4 3.8 all-to-all-start.1
  165.2 1.5 collective-permute-start.6
  167.3 4.0 collective-permute-done.4.refs_6_
  171.3 2.5 collective-permute-done.5.refs_7_
  173.8 1.1 copy-done.13
  175.9 1.3 copy-done.2
  177.2 12.2 %project.2 = f32[128,3584]{1,0:T(8,128)} custom-call(s32[336]{0:T(512)S(1)} %get-tuple-element.78.slots, s32[336]{0:T(512)S(1)} %get-tuple-element.76.rows, s32[1]{0:T(128)} %get-tuple-element.114.steps, bf16[64,128,128]{2,1,0:T(8,128)(2,1)} %all-gather.2.cloned.1.call-done.tok_ref, bf16[48,128,128]{2,1,0:T(8,128)(2,1)} %bitcast.97, ...), custom_call_target="tpu_custom_call" | custom-call | flops 1409286144 | bytes 46137344 | tf_op jit(solution)/shard_map/project/pallas_call | solution.py:235
  189.3 1.1 copy-done.4
  190.4 5.0 all-to-all-done.1
  195.4 1.5 collective-permute-start.9
  196.9 5.9 collective-permute-done.6.refs_1_.refs_2_
  203.3 26.6 %collective-permute-done.9.refs_5_.refs_6_ = bf16[40,128,128]{2,1,0:T(8,128)(2,1)S(1)} collective-permute-done((bf16[40,128,128]{2,1,0:T(8,128)(2,1)S(1)}, bf16[40,128,128]{2,1,0:T(8,128)(2,1)S(1)}, u32[]{:S(2)}, u32[]{:S(2)}) %collective-permute-start.9) | collective-permute-done | bytes 1310752 | tf_op jit(solution)/shard_map/ppermute | solution.py:171
  229.9 3.0 collective-permute-done.11.refs_7_.refs_8_
  232.9 1.1 copy-done.12
  235.0 22.3 %project.3 = f32[128,3584]{1,0:T(8,128)} custom-call(s32[336]{0:T(512)S(1)} %get-tuple-element.79.slots, s32[336]{0:T(512)S(1)} %get-tuple-element.77.rows, s32[1]{0:T(128)} %get-tuple-element.115.steps, bf16[64,128,128]{2,1,0:T(8,128)(2,1)} %all-gather.2.cloned.1.call-done.tok_ref, bf16[48,128,128]{2,1,0:T(8,128)(2,1)} %bitcast.14.refs_0_.refs_1_, ...), custom_call_target="tpu_custom_call" | custom-call | flops 1409286144 | bytes 46137344 | tf_op jit(solution)/shard_map/project/pallas_call | solution.py:235
  257.4 3.6 fusion.10
  260.9 19.3 %pull_back.2 = (f32[64,128,128]{2,1,0:T(8,128)}, bf16[88,128,128]{2,1,0:T(8,128)(2,1)}, bf16[88,128,128]{2,1,0:T(8,128)(2,1)}, bf16[88,128,128]{2,1,0:T(8,128)(2,1)}, bf16[88,128,128]{2,1,0:T(8,128)(2,1)}) custom-call(s32[336]{0:T(512)S(1)} %get-tuple-element.78.slots, s32[336]{0:T(512)S(1)} %get-tuple-element.74.targets, s32[336]{0:T(512)S(1)} %get-tuple-element.76.rows, ...), custom_call_target="tpu_custom_call" | custom-call | flops 2818572288 | bytes 69206016 | tf_op jit(solution)/shard_map/pull_back/pallas_call | solution.py:280
  280.8 5.0 collective-permute-done.12
  285.8 3.0 add_convert_fusion.3
  288.8 1.5 collective-permute-start.17
  290.4 32.8 %pull_back.3 = (bf16[64,128,128]{2,1,0:T(8,128)(2,1)}, bf16[88,128,128]{2,1,0:T(8,128)(2,1)}, bf16[88,128,128]{2,1,0:T(8,128)(2,1)}, bf16[88,128,128]{2,1,0:T(8,128)(2,1)}, bf16[88,128,128]{2,1,0:T(8,128)(2,1)}) custom-call(s32[336]{0:T(512)S(1)} %get-tuple-element.79.slots, s32[336]{0:T(512)S(1)} %get-tuple-element.75.targets, ...), custom_call_target="tpu_custom_call" | custom-call | flops 2818572288 | bytes 69206016 | tf_op jit(solution)/shard_map/pull_back/pallas_call | solution.py:280
  323.3 30.2 %collective-permute-done.17 = bf16[88,128,128]{2,1,0:T(8,128)(2,1)} collective-permute-done((bf16[88,128,128]{2,1,0:T(8,128)(2,1)S(1)}, bf16[88,128,128]{2,1,0:T(8,128)(2,1)}, u32[]{:S(2)}, u32[]{:S(2)}) %collective-permute-start.17) | collective-permute-done | bytes 2883616 | tf_op jit(solution)/shard_map/ppermute | solution.py:171
  353.5 5.2 add_convert_fusion
  358.7 9.1 %all-to-all-start.5 = ((bf16[8,11,128,128]{3,2,1,0:T(8,128)(2,1)}), bf16[8,11,128,128]{3,2,1,0:T(8,128)(2,1)S(1)}, u32[]{:S(2)}, u32[]{:S(2)}) async-start(bf16[8,11,128,128]{3,2,1,0:T(8,128)(2,1)} %bitcast.32), calls=%async_computation.6 | async-start | bytes 5767168 | tf_op jit(solution)/shard_map/all_to_all | solution.py:180
  367.8 4.0 add_convert_fusion.2
  371.8 1.5 collective-permute-start.15
  373.4 63.4 %collective-permute-done.15 = bf16[88,128,128]{2,1,0:T(8,128)(2,1)S(1)} collective-permute-done((bf16[88,128,128]{2,1,0:T(8,128)(2,1)S(1)}, bf16[88,128,128]{2,1,0:T(8,128)(2,1)S(1)}, u32[]{:S(2)}, u32[]{:S(2)}) %collective-permute-start.15) | collective-permute-done | bytes 2883616 | tf_op jit(solution)/shard_map/ppermute | solution.py:171
  436.7 4.0 add_convert_fusion.1
  440.8 1.6 copy-done.7
  442.3 6.0 all-to-all-start.4
  449.8 0.8 gather_fusion.6
  450.6 0.8 gather_fusion.4
  452.2 5.1 fusion.29
  457.3 5.0 fusion.28
  462.3 2.6 gather_fusion.7
  465.0 1.5 collective-permute-start.18
  466.5 63.8 %all-to-all-done.4 = bf16[8,11,128,128]{3,2,1,0:T(8,128)(2,1)} async-done(((bf16[8,11,128,128]{3,2,1,0:T(8,128)(2,1)}), bf16[8,11,128,128]{3,2,1,0:T(8,128)(2,1)}, u32[]{:S(2)}, u32[]{:S(2)}) %all-to-all-start.4) | async-done | bytes 2883616 | tf_op jit(solution)/shard_map/all_to_all | solution.py:180
  530.3 3.7 gather_fusion.5
  534.0 23.0 %reduce-scatter.2.cloned.1.call-done = bf16[8,128,128]{2,1,0:T(8,128)(2,1)} async-done(((bf16[64,128,128]{2,1,0:T(8,128)(2,1)}), bf16[8,128,128]{2,1,0:T(8,128)(2,1)}) %reduce-scatter.2.cloned.1.call-update) | async-done | bytes 262160 | tf_op jit(solution)/shard_map/reduce_scatter | solution.py:321
  557.0 1.5 collective-permute-start.21
  559.0 28.4 %collective-permute-done.21.refs_5_ = bf16[42,128,128]{2,1,0:T(8,128)(2,1)} collective-permute-done((bf16[42,128,128]{2,1,0:T(8,128)(2,1)}, bf16[42,128,128]{2,1,0:T(8,128)(2,1)}, u32[]{:S(2)}, u32[]{:S(2)}) %collective-permute-start.21) | collective-permute-done | bytes 1376288 | tf_op jit(solution)/shard_map/ppermute | solution.py:171
  587.6 1.1 copy.32
  588.7 0.9 copy.33
  589.6 1.4 collective-permute-done.23.refs_7_
  590.9 14.1 %collect.1 = f32[2,168,128,128]{3,2,1,0:T(8,128)} custom-call(s32[336]{0:T(512)S(1)} %pad_add_fusion.slots, bf16[42,128,128]{2,1,0:T(8,128)(2,1)S(1)} %gather_fusion.7, bf16[42,128,128]{2,1,0:T(8,128)(2,1)S(1)} %collective-permute-done.18.refs_1_, bf16[42,128,128]{2,1,0:T(8,128)(2,1)} %collective-permute-done.19.refs_2_, ...), custom_call_target="tpu_custom_call" | custom-call | tf_op jit(solution)/shard_map/collect/pallas_call | solution.py:328
  (131 shorter events, 12.1 us)
Async XLA Ops:
  9.0 6.5 %copy-start.20 = (s32[2,8,168]{2,1,0:T(8,128)}, s32[2,8,168]{2,1,0:T(8,128)S(1)}, u32[]{:S(2)}) copy-start(s32[2,8,168]{2,1,0:T(8,128)S(1)} %get-tuple-element.83) | copy-start | bytes 32260
  9.2 13.5 %copy-start.18 = (s32[2,8]{1,0:T(2,128)}, s32[2,8]{1,0:T(2,128)S(1)}, u32[]{:S(2)}) copy-start(s32[2,8]{1,0:T(2,128)S(1)} %and_select_fusion.9) | copy-start | bytes 196
  15.5 44.3 %all-to-all-start.2 = ((bf16[8,6,128,128]{3,2,1,0:T(8,128)(2,1)}), bf16[8,6,128,128]{3,2,1,0:T(8,128)(2,1)S(1)}, u32[]{:S(2)}, u32[]{:S(2)}) async-start(bf16[8,6,128,128]{3,2,1,0:T(8,128)(2,1)} %bitcast.101), calls=%async_computation.2 | async-start | bytes 3145728 | tf_op jit(solution)/shard_map/all_to_all | solution.py:180
  22.9 42.1 %copy-start.17 = (bf16[128,1024]{1,0:T(8,128)(2,1)S(1)}, bf16[128,1024]{1,0:T(8,128)(2,1)}, u32[]{:S(2)}) copy-start(bf16[128,1024]{1,0:T(8,128)(2,1)} %param.5) | copy-start | bytes 786436
  59.7 12.5 %copy-start.5 = (bf16[8,6,128,128]{3,2,1,0:T(8,128)(2,1)}, bf16[8,6,128,128]{3,2,1,0:T(8,128)(2,1)S(1)}, u32[]{:S(2)}) copy-start(bf16[8,6,128,128]{3,2,1,0:T(8,128)(2,1)S(1)} %all-to-all-done.2) | copy-start | bytes 4718596
  59.7 43.6 %all-to-all-start = ((bf16[8,5,128,128]{3,2,1,0:T(8,128)(2,1)}), bf16[8,5,128,128]{3,2,1,0:T(8,128)(2,1)S(1)}, u32[]{:S(2)}, u32[]{:S(2)}) async-start(bf16[8,5,128,128]{3,2,1,0:T(8,128)(2,1)} %bitcast.102), calls=%async_computation | async-start | bytes 2621440 | tf_op jit(solution)/shard_map/all_to_all | solution.py:180
  63.4 90.3 %all-gather.2.cloned.1.call-start = ((), (), s32[]{:S(2)}) async-start(), calls=%async_computation.7 | async-start | bytes 2359296 | tf_op jit(solution)/shard_map/all_gather | solution.py:194
  63.4 36.2 %collective-permute-start.1 = (bf16[48,128,128]{2,1,0:T(8,128)(2,1)S(1)}, bf16[48,128,128]{2,1,0:T(8,128)(2,1)}, u32[]{:S(2)}, u32[]{:S(2)}) collective-permute-start(bf16[48,128,128]{2,1,0:T(8,128)(2,1)S(1)} %bitcast.95), channel_id=1, source_target_pairs={{0,16},{8,24},{16,0},{24,8},{1,17},{9,25},{17,1},{25,9},{2,18},{10... | collective-permute-start | bytes 4718600 | tf_op jit(solution)/shard_map/ppermute | solution.py:171
  103.3 57.0 %all-to-all-start.3 = ((bf16[8,6,128,128]{3,2,1,0:T(8,128)(2,1)}), bf16[8,6,128,128]{3,2,1,0:T(8,128)(2,1)}, u32[]{:S(2)}, u32[]{:S(2)}) async-start(bf16[8,6,128,128]{3,2,1,0:T(8,128)(2,1)} %bitcast.100), calls=%async_computation.3 | async-start | bytes 3145728 | tf_op jit(solution)/shard_map/all_to_all | solution.py:180
  107.7 3.4 copy-start.21
  109.5 48.2 %collective-permute-start = (bf16[40,128,128]{2,1,0:T(8,128)(2,1)S(1)}, bf16[40,128,128]{2,1,0:T(8,128)(2,1)S(1)}, u32[]{:S(2)}, u32[]{:S(2)}) collective-permute-start(bf16[40,128,128]{2,1,0:T(8,128)(2,1)S(1)} %bitcast.87), channel_id=1, source_target_pairs={{0,16},{8,24},{16,0},{24,8},{1,17},{9,25},{17,1},{25,9},{2,18},{10... | collective-permute-start | bytes 3932168 | tf_op jit(solution)/shard_map/ppermute | solution.py:171
  157.7 2.6 copy-start.1
  160.4 35.0 %all-to-all-start.1 = ((bf16[8,5,128,128]{3,2,1,0:T(8,128)(2,1)}), bf16[8,5,128,128]{3,2,1,0:T(8,128)(2,1)S(1)}, u32[]{:S(2)}, u32[]{:S(2)}) async-start(bf16[8,5,128,128]{3,2,1,0:T(8,128)(2,1)} %bitcast.103), calls=%async_computation.1 | async-start | bytes 2621440 | tf_op jit(solution)/shard_map/all_to_all | solution.py:180
  164.1 9.7 %collective-permute-start.2 = (bf16[48,128,128]{2,1,0:T(8,128)(2,1)}, bf16[48,128,128]{2,1,0:T(8,128)(2,1)S(1)}, u32[]{:S(2)}, u32[]{:S(2)}) collective-permute-start(bf16[48,128,128]{2,1,0:T(8,128)(2,1)} %bitcast.96), channel_id=1, source_target_pairs={{0,8},{8,0},{16,24},{24,16},{1,9},{9,1},{17,25},{25,17},{2,10},{10... | collective-permute-start | bytes 4718600 | tf_op jit(solution)/shard_map/ppermute | solution.py:165
  164.2 9.6 %collective-permute-start.3 = (bf16[48,128,128]{2,1,0:T(8,128)(2,1)}, bf16[48,128,128]{2,1,0:T(8,128)(2,1)S(1)}, u32[]{:S(2)}, u32[]{:S(2)}) collective-permute-start(bf16[48,128,128]{2,1,0:T(8,128)(2,1)} %collective-permute-done.1.refs_1_), channel_id=1, source_target_pairs={{0,8},{8,0},{16,24},{24,16},{1,9},{9,1},{17,25},{25,17},{2,10},{10... | collective-permute-start | bytes 4718600 | tf_op jit(solution)/shard_map/ppermute | solution.py:165
  164.7 6.6 %collective-permute-start.4 = (bf16[40,128,128]{2,1,0:T(8,128)(2,1)S(1)}, bf16[40,128,128]{2,1,0:T(8,128)(2,1)S(1)}, u32[]{:S(2)}, u32[]{:S(2)}) collective-permute-start(bf16[40,128,128]{2,1,0:T(8,128)(2,1)S(1)} %bitcast.88), channel_id=1, source_target_pairs={{0,8},{8,0},{16,24},{24,16},{1,9},{9,1},{17,25},{25,17},{2,10},{10... | collective-permute-start | bytes 3932168 | tf_op jit(solution)/shard_map/ppermute | solution.py:165
  164.8 9.0 %collective-permute-start.5 = (bf16[40,128,128]{2,1,0:T(8,128)(2,1)}, bf16[40,128,128]{2,1,0:T(8,128)(2,1)S(1)}, u32[]{:S(2)}, u32[]{:S(2)}) collective-permute-start(bf16[40,128,128]{2,1,0:T(8,128)(2,1)} %copy-done.1), channel_id=1, source_target_pairs={{0,8},{8,0},{16,24},{24,16},{1,9},{9,1},{17,25},{25,17},{2,10},{10... | collective-permute-start | bytes 3932168 | tf_op jit(solution)/shard_map/ppermute | solution.py:165
  165.2 37.6 %collective-permute-start.6 = (bf16[48,128,128]{2,1,0:T(8,128)(2,1)}, bf16[48,128,128]{2,1,0:T(8,128)(2,1)}, u32[]{:S(2)}, u32[]{:S(2)}) collective-permute-start(bf16[48,128,128]{2,1,0:T(8,128)(2,1)} %bitcast.14.refs_0_.refs_1_), channel_id=1, source_target_pairs={{0,16},{8,24},{16,0},{24,8},{1,17},{9,25},{17,1},{25,9},{2,18},{10... | collective-permute-start | bytes 4718600 | tf_op jit(solution)/shard_map/ppermute | solution.py:171
  173.8 1.2 copy-start.13
  173.8 1.6 copy-start.10
  173.8 2.0 copy-start.11
  175.8 1.3 copy-start.2
  189.3 1.1 copy-start.4
  195.4 34.5 %collective-permute-start.9 = (bf16[40,128,128]{2,1,0:T(8,128)(2,1)S(1)}, bf16[40,128,128]{2,1,0:T(8,128)(2,1)S(1)}, u32[]{:S(2)}, u32[]{:S(2)}) collective-permute-start(bf16[40,128,128]{2,1,0:T(8,128)(2,1)S(1)} %bitcast.83), channel_id=1, source_target_pairs={{0,16},{8,24},{16,0},{24,8},{1,17},{9,25},{17,1},{25,9},{2,18},{10... | collective-permute-start | bytes 3932168 | tf_op jit(solution)/shard_map/ppermute | solution.py:171
  196.9 36.1 %collective-permute-start.7 = (bf16[48,128,128]{2,1,0:T(8,128)(2,1)}, bf16[48,128,128]{2,1,0:T(8,128)(2,1)S(1)}, u32[]{:S(2)}, u32[]{:S(2)}) collective-permute-start(bf16[48,128,128]{2,1,0:T(8,128)(2,1)} %bitcast.14.refs_0_.refs_1_), channel_id=1, source_target_pairs={{0,8},{8,0},{16,24},{24,16},{1,9},{9,1},{17,25},{25,17},{2,10},{10... | collective-permute-start | bytes 4718600 | tf_op jit(solution)/shard_map/ppermute | solution.py:165
  202.8 30.2 %collective-permute-start.8 = (bf16[48,128,128]{2,1,0:T(8,128)(2,1)}, bf16[48,128,128]{2,1,0:T(8,128)(2,1)S(1)}, u32[]{:S(2)}, u32[]{:S(2)}) collective-permute-start(bf16[48,128,128]{2,1,0:T(8,128)(2,1)} %collective-permute-done.6.refs_1_.refs_2_), channel_id=1, source_target_pairs={{0,8},{8,0},{16,24},{24,16},{1,9},{9,1},{17,25},{25,17},{2,10},{10... | collective-permute-start | bytes 4718600 | tf_op jit(solution)/shard_map/ppermute | solution.py:165
  202.8 27.1 %collective-permute-start.10 = (bf16[40,128,128]{2,1,0:T(8,128)(2,1)S(1)}, bf16[40,128,128]{2,1,0:T(8,128)(2,1)S(1)}, u32[]{:S(2)}, u32[]{:S(2)}) collective-permute-start(bf16[40,128,128]{2,1,0:T(8,128)(2,1)S(1)} %bitcast.84), channel_id=1, source_target_pairs={{0,8},{8,0},{16,24},{24,16},{1,9},{9,1},{17,25},{25,17},{2,10},{10... | collective-permute-start | bytes 3932168 | tf_op jit(solution)/shard_map/ppermute | solution.py:165
  229.9 3.0 collective-permute-start.11
  229.9 27.4 %copy-start = (bf16[40,128,128]{2,1,0:T(8,128)(2,1)}, bf16[40,128,128]{2,1,0:T(8,128)(2,1)S(1)}, u32[]{:S(2)}) copy-start(bf16[40,128,128]{2,1,0:T(8,128)(2,1)S(1)} %collective-permute-done.10.refs_6_.refs_7_) | copy-start | bytes 3932164
  232.9 1.1 copy-start.12
  232.9 1.7 copy-start.8
  232.9 2.1 copy-start.9
  235.0 22.3 %copy-start.6 = (f32[128,3584]{1,0:T(8,128)S(1)}, f32[128,3584]{1,0:T(8,128)}, u32[]{:S(2)}) copy-start(f32[128,3584]{1,0:T(8,128)} %project.2) | copy-start | bytes 5505028
  235.0 22.3 %copy-start.16 = (bf16[128,3584]{1,0:T(8,128)(2,1)S(1)}, bf16[128,3584]{1,0:T(8,128)(2,1)}, u32[]{:S(2)}) copy-start(bf16[128,3584]{1,0:T(8,128)(2,1)} %param.6) | copy-start | bytes 2752516
  257.3 3.6 copy-start.3
  280.2 5.6 collective-permute-start.12
  280.4 42.9 %collective-permute-start.16 = (bf16[88,128,128]{2,1,0:T(8,128)(2,1)}, bf16[88,128,128]{2,1,0:T(8,128)(2,1)S(1)}, u32[]{:S(2)}, u32[]{:S(2)}) collective-permute-start(bf16[88,128,128]{2,1,0:T(8,128)(2,1)} %get-tuple-element.56), channel_id=1, source_target_pairs={{0,8},{8,0},{16,24},{24,16},{1,9},{9,1},{17,25},{25,17},{2,10},{10... | collective-permute-start | bytes 8650760 | tf_op jit(solution)/shard_map/ppermute | solution.py:165
  288.8 64.7 %collective-permute-start.17 = (bf16[88,128,128]{2,1,0:T(8,128)(2,1)S(1)}, bf16[88,128,128]{2,1,0:T(8,128)(2,1)}, u32[]{:S(2)}, u32[]{:S(2)}) collective-permute-start(bf16[88,128,128]{2,1,0:T(8,128)(2,1)S(1)} %add_convert_fusion.3), channel_id=1, source_target_pairs={{0,16},{8,24},{16,0},{24,8},{1,17},{9,25},{17,1},{25,9},{2,18},{10... | collective-permute-start | bytes 8650760 | tf_op jit(solution)/shard_map/ppermute | solution.py:171
  290.4 63.2 %copy-start.14 = (bf16[88,128,128]{2,1,0:T(8,128)(2,1)S(1)}, bf16[88,128,128]{2,1,0:T(8,128)(2,1)}, u32[]{:S(2)}) copy-start(bf16[88,128,128]{2,1,0:T(8,128)(2,1)} %get-tuple-element.55) | copy-start | bytes 8650756
  323.2 44.6 %collective-permute-start.14 = (bf16[88,128,128]{2,1,0:T(8,128)(2,1)}, bf16[88,128,128]{2,1,0:T(8,128)(2,1)}, u32[]{:S(2)}, u32[]{:S(2)}) collective-permute-start(bf16[88,128,128]{2,1,0:T(8,128)(2,1)} %get-tuple-element.52), channel_id=1, source_target_pairs={{0,8},{8,0},{16,24},{24,16},{1,9},{9,1},{17,25},{25,17},{2,10},{10... | collective-permute-start | bytes 8650760 | tf_op jit(solution)/shard_map/ppermute | solution.py:165
  358.7 82.1 %all-to-all-start.5 = ((bf16[8,11,128,128]{3,2,1,0:T(8,128)(2,1)}), bf16[8,11,128,128]{3,2,1,0:T(8,128)(2,1)S(1)}, u32[]{:S(2)}, u32[]{:S(2)}) async-start(bf16[8,11,128,128]{3,2,1,0:T(8,128)(2,1)} %bitcast.32), calls=%async_computation.6 | async-start | bytes 5767168 | tf_op jit(solution)/shard_map/all_to_all | solution.py:180
  367.8 5.6 collective-permute-start.13
  367.8 68.9 %copy-start.15 = (bf16[88,128,128]{2,1,0:T(8,128)(2,1)S(1)}, bf16[88,128,128]{2,1,0:T(8,128)(2,1)}, u32[]{:S(2)}) copy-start(bf16[88,128,128]{2,1,0:T(8,128)(2,1)} %get-tuple-element.49) | copy-start | bytes 8650756
  371.8 64.9 %collective-permute-start.15 = (bf16[88,128,128]{2,1,0:T(8,128)(2,1)S(1)}, bf16[88,128,128]{2,1,0:T(8,128)(2,1)S(1)}, u32[]{:S(2)}, u32[]{:S(2)}) collective-permute-start(bf16[88,128,128]{2,1,0:T(8,128)(2,1)S(1)} %add_convert_fusion.2), channel_id=1, source_target_pairs={{0,16},{8,24},{16,0},{24,8},{1,17},{9,25},{17,1},{25,9},{2,18},{10... | collective-permute-start | bytes 8650760 | tf_op jit(solution)/shard_map/ppermute | solution.py:171
  440.8 1.6 copy-start.7
  442.3 88.0 %all-to-all-start.4 = ((bf16[8,11,128,128]{3,2,1,0:T(8,128)(2,1)}), bf16[8,11,128,128]{3,2,1,0:T(8,128)(2,1)}, u32[]{:S(2)}, u32[]{:S(2)}) async-start(bf16[8,11,128,128]{3,2,1,0:T(8,128)(2,1)} %bitcast.15), calls=%async_computation.4 | async-start | bytes 5767168 | tf_op jit(solution)/shard_map/all_to_all | solution.py:180
  448.3 3.1 copy-start.19
  448.3 108.7 %reduce-scatter.2.cloned.1.call-start = ((), (), s32[]{:S(2)}) async-start(), calls=%async_computation.8 | async-start | bytes 2359296 | tf_op jit(solution)/shard_map/reduce_scatter | solution.py:321
  465.0 93.5 %collective-permute-start.18 = (bf16[42,128,128]{2,1,0:T(8,128)(2,1)S(1)}, bf16[42,128,128]{2,1,0:T(8,128)(2,1)S(1)}, u32[]{:S(2)}, u32[]{:S(2)}) collective-permute-start(bf16[42,128,128]{2,1,0:T(8,128)(2,1)S(1)} %gather_fusion.7), channel_id=1, source_target_pairs={{0,16},{8,24},{16,0},{24,8},{1,17},{9,25},{17,1},{25,9},{2,18},{10... | collective-permute-start | bytes 4128776 | tf_op jit(solution)/shard_map/ppermute | solution.py:171
  557.0 30.4 %collective-permute-start.21 = (bf16[42,128,128]{2,1,0:T(8,128)(2,1)}, bf16[42,128,128]{2,1,0:T(8,128)(2,1)}, u32[]{:S(2)}, u32[]{:S(2)}) collective-permute-start(bf16[42,128,128]{2,1,0:T(8,128)(2,1)} %gather_fusion.5), channel_id=1, source_target_pairs={{0,16},{8,24},{16,0},{24,8},{1,17},{9,25},{17,1},{25,9},{2,18},{10... | collective-permute-start | bytes 4128776 | tf_op jit(solution)/shard_map/ppermute | solution.py:171
  558.5 31.1 %collective-permute-start.19 = (bf16[42,128,128]{2,1,0:T(8,128)(2,1)S(1)}, bf16[42,128,128]{2,1,0:T(8,128)(2,1)}, u32[]{:S(2)}, u32[]{:S(2)}) collective-permute-start(bf16[42,128,128]{2,1,0:T(8,128)(2,1)S(1)} %gather_fusion.7), channel_id=1, source_target_pairs={{0,8},{8,0},{16,24},{24,16},{1,9},{9,1},{17,25},{25,17},{2,10},{10... | collective-permute-start | bytes 4128776 | tf_op jit(solution)/shard_map/ppermute | solution.py:165
  558.5 31.0 %collective-permute-start.20 = (bf16[42,128,128]{2,1,0:T(8,128)(2,1)S(1)}, bf16[42,128,128]{2,1,0:T(8,128)(2,1)}, u32[]{:S(2)}, u32[]{:S(2)}) collective-permute-start(bf16[42,128,128]{2,1,0:T(8,128)(2,1)S(1)} %collective-permute-done.18.refs_1_), channel_id=1, source_target_pairs={{0,8},{8,0},{16,24},{24,16},{1,9},{9,1},{17,25},{25,17},{2,10},{10... | collective-permute-start | bytes 4128776 | tf_op jit(solution)/shard_map/ppermute | solution.py:165
  559.0 30.5 %collective-permute-start.22 = (bf16[42,128,128]{2,1,0:T(8,128)(2,1)}, bf16[42,128,128]{2,1,0:T(8,128)(2,1)}, u32[]{:S(2)}, u32[]{:S(2)}) collective-permute-start(bf16[42,128,128]{2,1,0:T(8,128)(2,1)} %gather_fusion.5), channel_id=1, source_target_pairs={{0,8},{8,0},{16,24},{24,16},{1,9},{9,1},{17,25},{25,17},{2,10},{10... | collective-permute-start | bytes 4128776 | tf_op jit(solution)/shard_map/ppermute | solution.py:165
  587.5 3.5 collective-permute-start.23
Sparse Core Ops, SparseCore 0:
  66.9 86.7 all-gather.1
  452.7 104.2 reduce-scatter.1

commit v4 on v3

--- a/solution.py
+++ b/solution.py
@@ -319,8 +319,8 @@
     gate_back = pack(0, total_of(gate_pieces, gate_pairs))
     up_back = pack(1, total_of(up_pieces, pairs_of(up_pieces)))
     mine = lax.psum_scatter(terms, "mp", scatter_dimension=0, tiled=True)
-    up_back, mine = lax.optimization_barrier((up_back, mine))
     home_pieces = spread(gate_back) + spread(up_back)
+    home_pieces[-1], mine = lax.optimization_barrier((home_pieces[-1], mine))
     input_grad = jnp.transpose(mine, (1, 0, 2)).reshape(tokens.shape)
 
     home = piece_of(tile_ids) * packed + tile_ids // groups

time: 613 us -> 638 us (1.041)
  Pallas kernels: 101 us -> 123 us
  waiting for transfers between devices: 345 us -> 354 us
    ppermute x8, waiting for transfers between devices: 182 us -> 207 us  [shift_y(): return lax.ppermute(x, 'dp', pairs)]
    reduce_scatter x1, waiting for transfers between devices: 23 us -> 0.01 us  [per_device(): mine = lax.psum_scatter(terms, 'mp', scatter_dimension=0, tiled=True)]
    pallas_call x2, Pallas kernels: 52.1 us -> 64.8 us  [pull_back(): pl.pallas_call(functools.partial(backward_kernel, begin, piece_count, gro...]
    ppermute x16, waiting for transfers between devices: 15.8 us -> 26.5 us  [swap_cores(): return lax.ppermute(x, 'dp', pairs)]
    pallas_call x2, Pallas kernels: 34.5 us -> 44.4 us  [project(): pl.pallas_call(forward_kernel, out_shape=jax.ShapeDtypeStruct(cotangent.s...]
  transfers between devices with their start and end apart: 32 -> 32, of which waited for: 18 -> 19; matrix products, arithmetic and copies ran while one was open for 14% -> 12% of each run, Pallas kernels for 7% -> 3%
where the time goes in v4:
time: 638 us; the launch traced here: 637 us
  waiting for transfers between devices  354 us (55%)
  Pallas kernels  123 us (19%)
  other arithmetic  51.2 us (8%)
  local copies, waits for them, and re-layouts  48.9 us (8%)
  starting transfers between devices  44.2 us (7%)
  between operations  14.6 us (2%)
    ppermute x8, waiting for transfers between devices, shift_y(): return lax.ppermute(x, 'dp', pairs)  207 us
    all_to_all x6, waiting for transfers between devices, exchange(): lax.all_to_all(x.reshape(members, -1, size, size), 'mp', split_axis=0, co...  102 us
    pallas_call x2, Pallas kernels, pull_back(): pl.pallas_call(functools.partial(backward_kernel, begin, piece_count, gro...  64.8 us
    pallas_call x2, Pallas kernels, project(): pl.pallas_call(forward_kernel, out_shape=jax.ShapeDtypeStruct(cotangent.s...  44.4 us
    all_to_all x6, starting transfers between devices, exchange(): lax.all_to_all(x.reshape(members, -1, size, size), 'mp', split_axis=0, co...  28.5 us
    ppermute x16, waiting for transfers between devices, swap_cores(): return lax.ppermute(x, 'dp', pairs)  26.5 us
    gather x4, local copies, waits for them, and re-layouts, send(): picked = jnp.take(flat_tiles, source.reshape(-1), axis=0, mode='clip')  24.3 us
    reduce_sum x1, other arithmetic, per_device(): jnp.sum(jnp.where(chosen, tile_rows[:, None, None, :], 0), axis=3)  17.7 us
  transfers between devices with their start and end apart: 32, of which 19 were waited for; matrix products, arithmetic and copies ran while one was open for 12% of the time, Pallas kernels for 3%

profile of v4, /device:TPU:0, one launch (start us, length us, event | category | flops | bytes accessed | tf_op | source)
XLA Modules:
  0.0 636.8 jit_solution(15159648687313320798)
XLA Ops:
  7.2 0.7 compare_and_fusion.1
  8.0 0.7 broadcast_subtract_fusion
  9.4 6.1 gather_fusion.3
  15.5 7.3 %all-to-all-start.2 = ((bf16[8,6,128,128]{3,2,1,0:T(8,128)(2,1)}), bf16[8,6,128,128]{3,2,1,0:T(8,128)(2,1)S(1)}, u32[]{:S(2)}, u32[]{:S(2)}) async-start(bf16[8,6,128,128]{3,2,1,0:T(8,128)(2,1)} %bitcast.101), calls=%async_computation.2 | async-start | bytes 3145728 | tf_op jit(solution)/shard_map/all_to_all | solution.py:180
  22.9 6.0 gather_fusion.1
  28.9 30.8 %all-to-all-done.2 = bf16[8,6,128,128]{3,2,1,0:T(8,128)(2,1)S(1)} async-done(((bf16[8,6,128,128]{3,2,1,0:T(8,128)(2,1)}), bf16[8,6,128,128]{3,2,1,0:T(8,128)(2,1)S(1)}, u32[]{:S(2)}, u32[]{:S(2)}) %all-to-all-start.2) | async-done | bytes 1572896 | tf_op jit(solution)/shard_map/all_to_all | solution.py:180
  59.7 3.6 all-to-all-start
  63.4 1.6 collective-permute-start.1
  65.2 0.9 copy.25
  66.1 6.1 gather_fusion.2
  72.3 27.3 %collective-permute-done.1.refs_1_ = bf16[48,128,128]{2,1,0:T(8,128)(2,1)} collective-permute-done((bf16[48,128,128]{2,1,0:T(8,128)(2,1)S(1)}, bf16[48,128,128]{2,1,0:T(8,128)(2,1)}, u32[]{:S(2)}, u32[]{:S(2)}) %collective-permute-start.1) | collective-permute-done | bytes 1572896 | tf_op jit(solution)/shard_map/ppermute | solution.py:171
  99.6 3.7 all-to-all-done
  103.3 4.3 all-to-all-start.3
  109.5 1.6 collective-permute-start
  111.1 17.7 %select_reduce_fusion = (s32[2,28,12]{0,2,1:T(8,128)S(1)}, s32[2,28,12]{0,2,1:T(8,128)S(1)}, s32[2,28,12]{0,2,1:T(8,128)S(1)}) fusion(s32[2,1344]{1,0:T(2,128)S(1)} %copy-done.19, s32[2,1344]{1,0:T(2,128)S(1)} %add_select_fusion.1, s32[2,1344]{1,0:T(2,128)S(1)} %get-tuple-element.80, s32[2,28,1344]{2,0,1:T(2,128)S(1)} %copy.28, pred[2,28,1344]{2,0,1:T(4,128)(4,1)S(1)} %copy.27), kind=kLoop, calls=%fused_computation.16 | loop fusion | flops 7223328 | bytes 416640 | tf_op jit(solution)/shard_map/reduce_sum | solution.py:216
  130.1 6.1 gather_fusion
  136.4 17.3 %all-gather.2.cloned.1.call-done.tok_ref = bf16[64,128,128]{2,1,0:T(8,128)(2,1)} async-done(((bf16[8,128,128]{2,1,0:T(8,128)(2,1)}), bf16[64,128,128]{2,1,0:T(8,128)(2,1)}) %all-gather.2.cloned.1.call-update) | async-done | bytes 2097168 | tf_op jit(solution)/shard_map/all_gather | solution.py:194
  153.6 4.1 copy.26
  157.7 2.6 all-to-all-done.3
  160.4 3.8 all-to-all-start.1
  165.2 1.5 collective-permute-start.6
  167.4 4.0 collective-permute-done.4.refs_6_
  171.3 2.5 collective-permute-done.5.refs_7_
  173.8 1.0 copy-done.12
  175.8 1.3 copy-done.2
  177.2 22.1 %project.2 = f32[128,3584]{1,0:T(8,128)} custom-call(s32[336]{0:T(512)S(1)} %get-tuple-element.78.slots, s32[336]{0:T(512)S(1)} %get-tuple-element.76.rows, s32[1]{0:T(128)} %get-tuple-element.114.steps, bf16[64,128,128]{2,1,0:T(8,128)(2,1)} %all-gather.2.cloned.1.call-done.tok_ref, bf16[48,128,128]{2,1,0:T(8,128)(2,1)} %bitcast.97, ...), custom_call_target="tpu_custom_call" | custom-call | flops 1409286144 | bytes 46137344 | tf_op jit(solution)/shard_map/project/pallas_call | solution.py:235
  199.3 1.1 copy-done.4
  200.4 1.5 collective-permute-start.9
  202.4 28.8 %collective-permute-done.9.refs_5_.refs_6_ = bf16[40,128,128]{2,1,0:T(8,128)(2,1)S(1)} collective-permute-done((bf16[40,128,128]{2,1,0:T(8,128)(2,1)S(1)}, bf16[40,128,128]{2,1,0:T(8,128)(2,1)S(1)}, u32[]{:S(2)}, u32[]{:S(2)}) %collective-permute-start.9) | collective-permute-done | bytes 1310752 | tf_op jit(solution)/shard_map/ppermute | solution.py:171
  231.2 3.0 collective-permute-done.11.refs_7_.refs_8_
  234.2 1.0 copy-done.11
  236.3 22.3 %project.3 = f32[128,3584]{1,0:T(8,128)} custom-call(s32[336]{0:T(512)S(1)} %get-tuple-element.79.slots, s32[336]{0:T(512)S(1)} %get-tuple-element.77.rows, s32[1]{0:T(128)} %get-tuple-element.115.steps, bf16[64,128,128]{2,1,0:T(8,128)(2,1)} %all-gather.2.cloned.1.call-done.tok_ref, bf16[48,128,128]{2,1,0:T(8,128)(2,1)} %bitcast.14.refs_0_.refs_1_, ...), custom_call_target="tpu_custom_call" | custom-call | flops 1409286144 | bytes 46137344 | tf_op jit(solution)/shard_map/project/pallas_call | solution.py:235
  258.7 3.6 fusion.10
  262.3 32.1 %pull_back.2 = (f32[64,128,128]{2,1,0:T(8,128)}, bf16[88,128,128]{2,1,0:T(8,128)(2,1)}, bf16[88,128,128]{2,1,0:T(8,128)(2,1)}, bf16[88,128,128]{2,1,0:T(8,128)(2,1)}, bf16[88,128,128]{2,1,0:T(8,128)(2,1)}) custom-call(s32[336]{0:T(512)S(1)} %get-tuple-element.78.slots, s32[336]{0:T(512)S(1)} %get-tuple-element.74.targets, s32[336]{0:T(512)S(1)} %get-tuple-element.76.rows, ...), custom_call_target="tpu_custom_call" | custom-call | flops 2818572288 | bytes 69206016 | tf_op jit(solution)/shard_map/pull_back/pallas_call | solution.py:280
  294.6 5.4 collective-permute-done.12
  300.0 4.6 add_convert_fusion.3
  304.6 32.6 %pull_back.3 = (bf16[64,128,128]{2,1,0:T(8,128)(2,1)}, bf16[88,128,128]{2,1,0:T(8,128)(2,1)}, bf16[88,128,128]{2,1,0:T(8,128)(2,1)}, bf16[88,128,128]{2,1,0:T(8,128)(2,1)}, bf16[88,128,128]{2,1,0:T(8,128)(2,1)}) custom-call(s32[336]{0:T(512)S(1)} %get-tuple-element.79.slots, s32[336]{0:T(512)S(1)} %get-tuple-element.75.targets, ...), custom_call_target="tpu_custom_call" | custom-call | flops 2818572288 | bytes 69206016 | tf_op jit(solution)/shard_map/pull_back/pallas_call | solution.py:280
  337.8 5.0 collective-permute-done.14
  342.8 3.2 add_convert_fusion.2
  346.0 1.5 collective-permute-start.15
  347.6 63.0 %collective-permute-done.15 = bf16[88,128,128]{2,1,0:T(8,128)(2,1)S(1)} collective-permute-done((bf16[88,128,128]{2,1,0:T(8,128)(2,1)S(1)}, bf16[88,128,128]{2,1,0:T(8,128)(2,1)S(1)}, u32[]{:S(2)}, u32[]{:S(2)}) %collective-permute-start.15) | collective-permute-done | bytes 2883616 | tf_op jit(solution)/shard_map/ppermute | solution.py:171
  410.6 4.0 add_convert_fusion.1
  414.6 3.6 all-to-all-start.4
  418.3 1.5 collective-permute-start.19
  419.8 3.9 collective-permute-done.18
  423.8 59.6 %collective-permute-done.19 = bf16[88,128,128]{2,1,0:T(8,128)(2,1)S(1)} collective-permute-done((bf16[88,128,128]{2,1,0:T(8,128)(2,1)}, bf16[88,128,128]{2,1,0:T(8,128)(2,1)S(1)}, u32[]{:S(2)}, u32[]{:S(2)}) %collective-permute-start.19) | collective-permute-done | bytes 2883616 | tf_op jit(solution)/shard_map/ppermute | solution.py:171
  483.4 5.8 add_convert_fusion
  489.2 5.9 all-to-all-start.5
  495.8 0.7 constant_dynamic-slice_fusion.1
  496.6 0.8 gather_fusion.6
  497.4 0.8 gather_fusion.4
  498.2 0.7 fusion.32
  498.9 4.9 fusion.29
  503.8 5.0 fusion.28
  508.8 1.9 gather_fusion.5
  510.7 1.5 collective-permute-start.16
  512.2 64.8 %all-to-all-done.5 = bf16[8,11,128,128]{3,2,1,0:T(8,128)(2,1)} async-done(((bf16[8,11,128,128]{3,2,1,0:T(8,128)(2,1)}), bf16[8,11,128,128]{3,2,1,0:T(8,128)(2,1)}, u32[]{:S(2)}, u32[]{:S(2)}) %all-to-all-start.5) | async-done | bytes 2883616 | tf_op jit(solution)/shard_map/all_to_all | solution.py:180
  577.1 2.6 gather_fusion.7
  579.7 1.5 collective-permute-start.20
  581.7 28.7 %collective-permute-done.20.refs_1_ = bf16[42,128,128]{2,1,0:T(8,128)(2,1)S(1)} collective-permute-done((bf16[42,128,128]{2,1,0:T(8,128)(2,1)S(1)}, bf16[42,128,128]{2,1,0:T(8,128)(2,1)S(1)}, u32[]{:S(2)}, u32[]{:S(2)}) %collective-permute-start.20) | collective-permute-done | bytes 1376288 | tf_op jit(solution)/shard_map/ppermute | solution.py:171
  611.0 1.1 copy.32
  612.2 0.9 copy.33
  613.0 2.6 collective-permute-done.22.refs_3_
  615.8 14.1 %collect.1 = f32[2,168,128,128]{3,2,1,0:T(8,128)} custom-call(s32[336]{0:T(512)S(1)} %pad_add_fusion.slots, bf16[42,128,128]{2,1,0:T(8,128)(2,1)S(1)} %gather_fusion.7, bf16[42,128,128]{2,1,0:T(8,128)(2,1)S(1)} %collective-permute-done.20.refs_1_, bf16[42,128,128]{2,1,0:T(8,128)(2,1)} %collective-permute-done.21.refs_2_, ...), custom_call_target="tpu_custom_call" | custom-call | tf_op jit(solution)/shard_map/collect/pallas_call | solution.py:328
  (127 shorter events, 11.8 us)
Async XLA Ops:
  9.0 6.5 %copy-start.18 = (s32[2,8,168]{2,1,0:T(8,128)}, s32[2,8,168]{2,1,0:T(8,128)S(1)}, u32[]{:S(2)}) copy-start(s32[2,8,168]{2,1,0:T(8,128)S(1)} %get-tuple-element.83) | copy-start | bytes 32260
  9.2 13.5 %copy-start.16 = (s32[2,8]{1,0:T(2,128)}, s32[2,8]{1,0:T(2,128)S(1)}, u32[]{:S(2)}) copy-start(s32[2,8]{1,0:T(2,128)S(1)} %and_select_fusion.9) | copy-start | bytes 196
  15.5 44.3 %all-to-all-start.2 = ((bf16[8,6,128,128]{3,2,1,0:T(8,128)(2,1)}), bf16[8,6,128,128]{3,2,1,0:T(8,128)(2,1)S(1)}, u32[]{:S(2)}, u32[]{:S(2)}) async-start(bf16[8,6,128,128]{3,2,1,0:T(8,128)(2,1)} %bitcast.101), calls=%async_computation.2 | async-start | bytes 3145728 | tf_op jit(solution)/shard_map/all_to_all | solution.py:180
  22.9 42.1 %copy-start.15 = (bf16[128,1024]{1,0:T(8,128)(2,1)S(1)}, bf16[128,1024]{1,0:T(8,128)(2,1)}, u32[]{:S(2)}) copy-start(bf16[128,1024]{1,0:T(8,128)(2,1)} %param.5) | copy-start | bytes 786436
  59.7 12.5 %copy-start.5 = (bf16[8,6,128,128]{3,2,1,0:T(8,128)(2,1)}, bf16[8,6,128,128]{3,2,1,0:T(8,128)(2,1)S(1)}, u32[]{:S(2)}) copy-start(bf16[8,6,128,128]{3,2,1,0:T(8,128)(2,1)S(1)} %all-to-all-done.2) | copy-start | bytes 4718596
  59.7 43.6 %all-to-all-start = ((bf16[8,5,128,128]{3,2,1,0:T(8,128)(2,1)}), bf16[8,5,128,128]{3,2,1,0:T(8,128)(2,1)S(1)}, u32[]{:S(2)}, u32[]{:S(2)}) async-start(bf16[8,5,128,128]{3,2,1,0:T(8,128)(2,1)} %bitcast.102), calls=%async_computation | async-start | bytes 2621440 | tf_op jit(solution)/shard_map/all_to_all | solution.py:180
  63.4 90.3 %all-gather.2.cloned.1.call-start = ((), (), s32[]{:S(2)}) async-start(), calls=%async_computation.7 | async-start | bytes 2359296 | tf_op jit(solution)/shard_map/all_gather | solution.py:194
  63.4 36.2 %collective-permute-start.1 = (bf16[48,128,128]{2,1,0:T(8,128)(2,1)S(1)}, bf16[48,128,128]{2,1,0:T(8,128)(2,1)}, u32[]{:S(2)}, u32[]{:S(2)}) collective-permute-start(bf16[48,128,128]{2,1,0:T(8,128)(2,1)S(1)} %bitcast.95), channel_id=1, source_target_pairs={{0,16},{8,24},{16,0},{24,8},{1,17},{9,25},{17,1},{25,9},{2,18},{10... | collective-permute-start | bytes 4718600 | tf_op jit(solution)/shard_map/ppermute | solution.py:171
  103.3 57.0 %all-to-all-start.3 = ((bf16[8,6,128,128]{3,2,1,0:T(8,128)(2,1)}), bf16[8,6,128,128]{3,2,1,0:T(8,128)(2,1)}, u32[]{:S(2)}, u32[]{:S(2)}) async-start(bf16[8,6,128,128]{3,2,1,0:T(8,128)(2,1)} %bitcast.100), calls=%async_computation.3 | async-start | bytes 3145728 | tf_op jit(solution)/shard_map/all_to_all | solution.py:180
  107.7 3.4 copy-start.19
  109.5 48.2 %collective-permute-start = (bf16[40,128,128]{2,1,0:T(8,128)(2,1)S(1)}, bf16[40,128,128]{2,1,0:T(8,128)(2,1)S(1)}, u32[]{:S(2)}, u32[]{:S(2)}) collective-permute-start(bf16[40,128,128]{2,1,0:T(8,128)(2,1)S(1)} %bitcast.87), channel_id=1, source_target_pairs={{0,16},{8,24},{16,0},{24,8},{1,17},{9,25},{17,1},{25,9},{2,18},{10... | collective-permute-start | bytes 3932168 | tf_op jit(solution)/shard_map/ppermute | solution.py:171
  157.7 2.6 copy-start.1
  160.4 40.0 %all-to-all-start.1 = ((bf16[8,5,128,128]{3,2,1,0:T(8,128)(2,1)}), bf16[8,5,128,128]{3,2,1,0:T(8,128)(2,1)S(1)}, u32[]{:S(2)}, u32[]{:S(2)}) async-start(bf16[8,5,128,128]{3,2,1,0:T(8,128)(2,1)} %bitcast.103), calls=%async_computation.1 | async-start | bytes 2621440 | tf_op jit(solution)/shard_map/all_to_all | solution.py:180
  164.1 9.7 %collective-permute-start.2 = (bf16[48,128,128]{2,1,0:T(8,128)(2,1)}, bf16[48,128,128]{2,1,0:T(8,128)(2,1)S(1)}, u32[]{:S(2)}, u32[]{:S(2)}) collective-permute-start(bf16[48,128,128]{2,1,0:T(8,128)(2,1)} %bitcast.96), channel_id=1, source_target_pairs={{0,8},{8,0},{16,24},{24,16},{1,9},{9,1},{17,25},{25,17},{2,10},{10... | collective-permute-start | bytes 4718600 | tf_op jit(solution)/shard_map/ppermute | solution.py:165
  164.2 9.6 %collective-permute-start.3 = (bf16[48,128,128]{2,1,0:T(8,128)(2,1)}, bf16[48,128,128]{2,1,0:T(8,128)(2,1)S(1)}, u32[]{:S(2)}, u32[]{:S(2)}) collective-permute-start(bf16[48,128,128]{2,1,0:T(8,128)(2,1)} %collective-permute-done.1.refs_1_), channel_id=1, source_target_pairs={{0,8},{8,0},{16,24},{24,16},{1,9},{9,1},{17,25},{25,17},{2,10},{10... | collective-permute-start | bytes 4718600 | tf_op jit(solution)/shard_map/ppermute | solution.py:165
  164.7 6.6 %collective-permute-start.4 = (bf16[40,128,128]{2,1,0:T(8,128)(2,1)S(1)}, bf16[40,128,128]{2,1,0:T(8,128)(2,1)S(1)}, u32[]{:S(2)}, u32[]{:S(2)}) collective-permute-start(bf16[40,128,128]{2,1,0:T(8,128)(2,1)S(1)} %bitcast.88), channel_id=1, source_target_pairs={{0,8},{8,0},{16,24},{24,16},{1,9},{9,1},{17,25},{25,17},{2,10},{10... | collective-permute-start | bytes 3932168 | tf_op jit(solution)/shard_map/ppermute | solution.py:165
  164.8 9.0 %collective-permute-start.5 = (bf16[40,128,128]{2,1,0:T(8,128)(2,1)}, bf16[40,128,128]{2,1,0:T(8,128)(2,1)S(1)}, u32[]{:S(2)}, u32[]{:S(2)}) collective-permute-start(bf16[40,128,128]{2,1,0:T(8,128)(2,1)} %copy-done.1), channel_id=1, source_target_pairs={{0,8},{8,0},{16,24},{24,16},{1,9},{9,1},{17,25},{25,17},{2,10},{10... | collective-permute-start | bytes 3932168 | tf_op jit(solution)/shard_map/ppermute | solution.py:165
  165.2 36.7 %collective-permute-start.6 = (bf16[48,128,128]{2,1,0:T(8,128)(2,1)}, bf16[48,128,128]{2,1,0:T(8,128)(2,1)}, u32[]{:S(2)}, u32[]{:S(2)}) collective-permute-start(bf16[48,128,128]{2,1,0:T(8,128)(2,1)} %bitcast.14.refs_0_.refs_1_), channel_id=1, source_target_pairs={{0,16},{8,24},{16,0},{24,8},{1,17},{9,25},{17,1},{25,9},{2,18},{10... | collective-permute-start | bytes 4718600 | tf_op jit(solution)/shard_map/ppermute | solution.py:171
  173.8 1.1 copy-start.12
  173.8 1.5 copy-start.9
  173.8 2.0 copy-start.10
  175.8 1.3 copy-start.2
  199.3 1.1 copy-start.4
  200.4 30.8 %collective-permute-start.9 = (bf16[40,128,128]{2,1,0:T(8,128)(2,1)S(1)}, bf16[40,128,128]{2,1,0:T(8,128)(2,1)S(1)}, u32[]{:S(2)}, u32[]{:S(2)}) collective-permute-start(bf16[40,128,128]{2,1,0:T(8,128)(2,1)S(1)} %bitcast.83), channel_id=1, source_target_pairs={{0,16},{8,24},{16,0},{24,8},{1,17},{9,25},{17,1},{25,9},{2,18},{10... | collective-permute-start | bytes 3932168 | tf_op jit(solution)/shard_map/ppermute | solution.py:171
  201.8 32.4 %collective-permute-start.7 = (bf16[48,128,128]{2,1,0:T(8,128)(2,1)}, bf16[48,128,128]{2,1,0:T(8,128)(2,1)S(1)}, u32[]{:S(2)}, u32[]{:S(2)}) collective-permute-start(bf16[48,128,128]{2,1,0:T(8,128)(2,1)} %bitcast.14.refs_0_.refs_1_), channel_id=1, source_target_pairs={{0,8},{8,0},{16,24},{24,16},{1,9},{9,1},{17,25},{25,17},{2,10},{10... | collective-permute-start | bytes 4718600 | tf_op jit(solution)/shard_map/ppermute | solution.py:165
  201.9 32.3 %collective-permute-start.8 = (bf16[48,128,128]{2,1,0:T(8,128)(2,1)}, bf16[48,128,128]{2,1,0:T(8,128)(2,1)S(1)}, u32[]{:S(2)}, u32[]{:S(2)}) collective-permute-start(bf16[48,128,128]{2,1,0:T(8,128)(2,1)} %collective-permute-done.6.refs_1_.refs_2_), channel_id=1, source_target_pairs={{0,8},{8,0},{16,24},{24,16},{1,9},{9,1},{17,25},{25,17},{2,10},{10... | collective-permute-start | bytes 4718600 | tf_op jit(solution)/shard_map/ppermute | solution.py:165
  202.4 28.9 %collective-permute-start.10 = (bf16[40,128,128]{2,1,0:T(8,128)(2,1)S(1)}, bf16[40,128,128]{2,1,0:T(8,128)(2,1)S(1)}, u32[]{:S(2)}, u32[]{:S(2)}) collective-permute-start(bf16[40,128,128]{2,1,0:T(8,128)(2,1)S(1)} %bitcast.84), channel_id=1, source_target_pairs={{0,8},{8,0},{16,24},{24,16},{1,9},{9,1},{17,25},{25,17},{2,10},{10... | collective-permute-start | bytes 3932168 | tf_op jit(solution)/shard_map/ppermute | solution.py:165
  231.2 3.0 collective-permute-start.11
  231.2 27.5 %copy-start = (bf16[40,128,128]{2,1,0:T(8,128)(2,1)}, bf16[40,128,128]{2,1,0:T(8,128)(2,1)S(1)}, u32[]{:S(2)}) copy-start(bf16[40,128,128]{2,1,0:T(8,128)(2,1)S(1)} %collective-permute-done.10.refs_6_.refs_7_) | copy-start | bytes 3932164
  234.2 1.1 copy-start.11
  234.2 1.6 copy-start.7
  234.2 2.1 copy-start.8
  236.3 22.3 %copy-start.6 = (f32[128,3584]{1,0:T(8,128)S(1)}, f32[128,3584]{1,0:T(8,128)}, u32[]{:S(2)}) copy-start(f32[128,3584]{1,0:T(8,128)} %project.2) | copy-start | bytes 5505028
  236.3 22.4 %copy-start.14 = (bf16[128,3584]{1,0:T(8,128)(2,1)S(1)}, bf16[128,3584]{1,0:T(8,128)(2,1)}, u32[]{:S(2)}) copy-start(bf16[128,3584]{1,0:T(8,128)(2,1)} %param.6) | copy-start | bytes 2752516
  258.7 3.6 copy-start.3
  294.4 5.6 collective-permute-start.12
  337.3 5.6 collective-permute-start.14
  337.5 10.1 %collective-permute-start.13 = (bf16[88,128,128]{2,1,0:T(8,128)(2,1)}, bf16[88,128,128]{2,1,0:T(8,128)(2,1)S(1)}, u32[]{:S(2)}, u32[]{:S(2)}) collective-permute-start(bf16[88,128,128]{2,1,0:T(8,128)(2,1)} %get-tuple-element.50), channel_id=1, source_target_pairs={{0,8},{8,0},{16,24},{24,16},{1,9},{9,1},{17,25},{25,17},{2,10},{10... | collective-permute-start | bytes 8650760 | tf_op jit(solution)/shard_map/ppermute | solution.py:165
  342.8 67.8 %copy-start.13 = (bf16[88,128,128]{2,1,0:T(8,128)(2,1)S(1)}, bf16[88,128,128]{2,1,0:T(8,128)(2,1)}, u32[]{:S(2)}) copy-start(bf16[88,128,128]{2,1,0:T(8,128)(2,1)} %get-tuple-element.49) | copy-start | bytes 8650756
  346.0 64.6 %collective-permute-start.15 = (bf16[88,128,128]{2,1,0:T(8,128)(2,1)S(1)}, bf16[88,128,128]{2,1,0:T(8,128)(2,1)S(1)}, u32[]{:S(2)}, u32[]{:S(2)}) collective-permute-start(bf16[88,128,128]{2,1,0:T(8,128)(2,1)S(1)} %add_convert_fusion.2), channel_id=1, source_target_pairs={{0,16},{8,24},{16,0},{24,8},{1,17},{9,25},{17,1},{25,9},{2,18},{10... | collective-permute-start | bytes 8650760 | tf_op jit(solution)/shard_map/ppermute | solution.py:171
  414.6 74.6 %all-to-all-start.4 = ((bf16[8,11,128,128]{3,2,1,0:T(8,128)(2,1)}), bf16[8,11,128,128]{3,2,1,0:T(8,128)(2,1)S(1)}, u32[]{:S(2)}, u32[]{:S(2)}) async-start(bf16[8,11,128,128]{3,2,1,0:T(8,128)(2,1)} %bitcast.15), calls=%async_computation.4 | async-start | bytes 5767168 | tf_op jit(solution)/shard_map/all_to_all | solution.py:180
  418.2 5.6 collective-permute-start.18
  418.3 65.1 %collective-permute-start.19 = (bf16[88,128,128]{2,1,0:T(8,128)(2,1)}, bf16[88,128,128]{2,1,0:T(8,128)(2,1)S(1)}, u32[]{:S(2)}, u32[]{:S(2)}) collective-permute-start(bf16[88,128,128]{2,1,0:T(8,128)(2,1)} %add_convert_fusion.3), channel_id=1, source_target_pairs={{0,16},{8,24},{16,0},{24,8},{1,17},{9,25},{17,1},{25,9},{2,18},{10... | collective-permute-start | bytes 8650760 | tf_op jit(solution)/shard_map/ppermute | solution.py:171
  489.2 87.8 %all-to-all-start.5 = ((bf16[8,11,128,128]{3,2,1,0:T(8,128)(2,1)}), bf16[8,11,128,128]{3,2,1,0:T(8,128)(2,1)}, u32[]{:S(2)}, u32[]{:S(2)}) async-start(bf16[8,11,128,128]{3,2,1,0:T(8,128)(2,1)} %bitcast.32), calls=%async_computation.6 | async-start | bytes 5767168 | tf_op jit(solution)/shard_map/all_to_all | solution.py:180
  495.1 3.1 copy-start.17
  495.1 115.9 %reduce-scatter.2.cloned.1.call-start = ((), (), s32[]{:S(2)}) async-start(), calls=%async_computation.8 | async-start | bytes 2359296 | tf_op jit(solution)/shard_map/reduce_scatter | solution.py:321
  510.7 70.5 %collective-permute-start.16 = (bf16[42,128,128]{2,1,0:T(8,128)(2,1)}, bf16[42,128,128]{2,1,0:T(8,128)(2,1)}, u32[]{:S(2)}, u32[]{:S(2)}) collective-permute-start(bf16[42,128,128]{2,1,0:T(8,128)(2,1)} %gather_fusion.5), channel_id=1, source_target_pairs={{0,16},{8,24},{16,0},{24,8},{1,17},{9,25},{17,1},{25,9},{2,18},{10... | collective-permute-start | bytes 4128776 | tf_op jit(solution)/shard_map/ppermute | solution.py:171
  579.7 30.7 %collective-permute-start.20 = (bf16[42,128,128]{2,1,0:T(8,128)(2,1)S(1)}, bf16[42,128,128]{2,1,0:T(8,128)(2,1)S(1)}, u32[]{:S(2)}, u32[]{:S(2)}) collective-permute-start(bf16[42,128,128]{2,1,0:T(8,128)(2,1)S(1)} %gather_fusion.7), channel_id=1, source_target_pairs={{0,16},{8,24},{16,0},{24,8},{1,17},{9,25},{17,1},{25,9},{2,18},{10... | collective-permute-start | bytes 4128776 | tf_op jit(solution)/shard_map/ppermute | solution.py:171
  581.2 29.8 %collective-permute-start.17 = (bf16[42,128,128]{2,1,0:T(8,128)(2,1)}, bf16[42,128,128]{2,1,0:T(8,128)(2,1)}, u32[]{:S(2)}, u32[]{:S(2)}) collective-permute-start(bf16[42,128,128]{2,1,0:T(8,128)(2,1)} %collective-permute-done.16.refs_5_), channel_id=1, source_target_pairs={{0,8},{8,0},{16,24},{24,16},{1,9},{9,1},{17,25},{25,17},{2,10},{10... | collective-permute-start | bytes 4128776 | tf_op jit(solution)/shard_map/ppermute | solution.py:165
  581.2 31.8 %collective-permute-start.21 = (bf16[42,128,128]{2,1,0:T(8,128)(2,1)S(1)}, bf16[42,128,128]{2,1,0:T(8,128)(2,1)}, u32[]{:S(2)}, u32[]{:S(2)}) collective-permute-start(bf16[42,128,128]{2,1,0:T(8,128)(2,1)S(1)} %gather_fusion.7), channel_id=1, source_target_pairs={{0,8},{8,0},{16,24},{24,16},{1,9},{9,1},{17,25},{25,17},{2,10},{10... | collective-permute-start | bytes 4128776 | tf_op jit(solution)/shard_map/ppermute | solution.py:165
  610.4 5.2 collective-permute-start.22
  610.4 5.4 collective-permute-start.23
Sparse Core Ops, SparseCore 0:
  66.9 86.7 all-gather.1
  499.5 104.3 reduce-scatter.1
